TPU v7x, 128 devices: a whole 4x4x4 slice. The times are simulated.
128 devices in a mesh: dp: 16 (over z, y_lo, core), blk: 8 (over x, y_hi).
Axes of the slice: x: 4, y: 4 (y_hi: 2, y_lo: 2; y = y_hi * 2 + y_lo), z: 4, core: 2. Of those that a mesh axis runs over, the one named last changes fastest.
Arguments:
- image_rows: bfloat16 [32, 1024, 1024], P('dp', 'blk'), may hold values from -6 to 6
- text_states: bfloat16 [128, 1024], replicated, may hold values from -6 to 6
- text_segment: int32 [128], replicated, may hold values from 0 to 7, never falling along the last dimension, each value on 1 to 32 neighbouring positions
- item_segment: int32 [32], P('dp'), may hold values from 0 to 7
- norm_gain: float32 [3, 1024], replicated, may hold values from 0.5 to 1.5
- norm_shift: float32 [3, 1024], replicated, may hold values from -2 to 2
- triple_weight: bfloat16 [1024, 3072], replicated, may hold values from -0.1875 to 0.1875
- output_weight: bfloat16 [1024, 1024], replicated, may hold values from -0.75 to 0.75
- query_weight: bfloat16 [1024, 1024], replicated, may hold values from -0.1875 to 0.1875
- memory_weight: bfloat16 [1024, 2048], replicated, may hold values from -0.1875 to 0.1875
- return_weight: bfloat16 [1024, 1024], replicated, may hold values from -0.75 to 0.75
- up_weight: bfloat16 [1024, 4096], replicated, may hold values from -0.1875 to 0.1875
- inner_bias: float32 [4096], replicated, may hold values from -2 to 2
- down_weight: bfloat16 [4096, 1024], replicated, may hold values from -0.09375 to 0.09375
- outer_bias: float32 [1024], replicated, may hold values from -2 to 2
- cotangent: bfloat16 [32, 1024, 1024], P('dp', 'blk'), may hold values from -6 to 6
Outputs:
- layer_output: bfloat16 [32, 1024, 1024], P('dp', 'blk')
- input_grad: float32 [32, 1024, 1024], P('dp', 'blk')
- text_grad: float32 [128, 1024], P(None, ('dp', 'blk'))
- gain_grad: float32 [3, 1024], P(None, ('dp', 'blk'))
- shift_grad: float32 [3, 1024], P(None, ('dp', 'blk'))
- triple_grad: float32 [1024, 3072], P(('dp', 'blk'))
- output_grad: float32 [1024, 1024], P(('dp', 'blk'))
- query_grad: float32 [1024, 1024], P(('dp', 'blk'))
- memory_grad: float32 [1024, 2048], P(('dp', 'blk'))
- return_grad: float32 [1024, 1024], P(('dp', 'blk'))
- up_grad: float32 [1024, 4096], P(('dp', 'blk'))
- inner_grad: float32 [4096], P(('dp', 'blk'))
- down_grad: float32 [4096, 1024], P(('dp', 'blk'))
- outer_grad: float32 [1024], P(('dp', 'blk'))
Inputs may be any that keep to these rules, and one draw needn't show every extreme that they name: `text_segment`: caption numbers never fall along the rows; each caption has 1 to 32 rows.
All inputs are finite; a program needn't handle non-finite values.
Results may differ from a plain program's by a relative error of at most 0.035.
Values may be sent and summed in bfloat16 or wider, within the bound.
No kernel may reach another device: no remote copies, remote signals or barrier semaphores. Data moves between devices by JAX's collectives and lax.ppermute only.
A program may use at most 256 MiB of HBM per device.

v0:
```python
import math

import jax
import jax.numpy as jnp
from jax import lax
from jax.sharding import PartitionSpec as P

DH = 64


epsilon = 1e-05
score_scale = 0.125
masked_value = -1e30


def in_one_piece(arrays, axis, dim, along):
    both = jnp.concatenate(arrays, axis=along)
    result, at, done = (lax.all_gather(both, axis, axis=dim, tiled=True), 0, [])
    for a in arrays:
        done.append(lax.slice_in_dim(result, at, at + a.shape[along], axis=along))
        at += a.shape[along]
    return tuple(done)


def side_by_side(arrays, axis, dim, along):
    ends, at = ([], 0)
    for a in arrays[:-1]:
        at += a.shape[along]
        ends.append(at)
    both = jnp.concatenate(arrays, axis=along)
    return tuple(
        jnp.split(lax.psum_scatter(both, axis, scatter_dimension=dim, tiled=True), ends, axis=along)
    )


def sent_together(arrays, axis, dim, along):
    widths = [math.prod(a.shape[along:]) for a in arrays]
    both = jnp.concatenate(
        [a.reshape(*a.shape[:along], w) for a, w in zip(arrays, widths)], axis=along
    )
    result = lax.psum_scatter(both, axis, scatter_dimension=dim, tiled=True)
    pieces = jnp.split(result, [sum(widths[:k]) for k in range(1, len(widths))], axis=along)
    return tuple(
        (b.reshape(*result.shape[:along], *a.shape[along:]) for a, b in zip(arrays, pieces))
    )


def split_up(x, dim, devices):
    before, after = (x.shape[:dim], x.shape[dim + 1 :])
    return jnp.moveaxis(x.reshape(*before, devices, -1, *after), dim, 0)


def one_scatter(arrays, axis, dims):
    devices = lax.axis_size(axis)
    pieces = [split_up(a, dim, devices) for a, dim in zip(arrays, dims)]
    lines = jnp.concatenate([b.reshape(devices, -1) for b in pieces], axis=1)
    rows = max(16, -(-lines.shape[1] // 1024) * 8)
    lines = jnp.pad(lines, ((0, 0), (0, rows * 128 - lines.shape[1]))).reshape(-1, 128)
    flat, at, done = (lax.psum_scatter(lines, axis, tiled=True).reshape(-1), 0, [])
    for b in pieces:
        part = b[0]
        done.append(flat[at : at + part.size].reshape(part.shape))
        at += part.size
    return tuple(done)


def layer_norm(values, gain_row, shift_row):
    average = jnp.mean(values, axis=-1, keepdims=True)
    centred = values - average
    variance = jnp.mean(centred * centred, axis=-1, keepdims=True)
    return centred * lax.rsqrt(variance + epsilon) * gain_row + shift_row


def narrow(values):
    return values.astype(jnp.bfloat16)


def matmul(left, right):
    return jnp.dot(left, right, preferred_element_type=jnp.float32)


def dot_left(left, right):
    return lax.dot_general(
        left, right, (((0,), (0,)), ((), ())), preferred_element_type=jnp.float32
    )


def dot_right(left, right):
    return lax.dot_general(
        left, right, (((1,), (1,)), ((), ())), preferred_element_type=jnp.float32
    )


def local(
    image_rows,
    text_states,
    text_segment,
    item_segment,
    norm_gain,
    norm_shift,
    triple_weight,
    output_weight,
    query_weight,
    memory_weight,
    return_weight,
    up_weight,
    inner_bias,
    down_weight,
    outer_bias,
    cotangent,
):
    item_count, block_rows, model_width = image_rows.shape
    tokens = item_count * block_rows
    text_rows = text_states.shape[0]
    head_count = model_width // DH
    cycle_size = lax.axis_size("blk")
    cycle_index = lax.axis_index("blk")
    full_rows = block_rows * cycle_size
    query_pos = cycle_index * block_rows + lax.iota(jnp.int32, block_rows)
    key_pos = lax.iota(jnp.int32, full_rows)
    causal = key_pos[None, :] <= query_pos[:, None]
    inputs = image_rows.astype(jnp.float32).reshape(tokens, model_width)
    normed_one, pull_one = jax.vjp(layer_norm, inputs, norm_gain[0], norm_shift[0])
    hidden_one = narrow(normed_one)
    triple = narrow(matmul(hidden_one, triple_weight))
    queries = triple[:, :model_width].reshape(item_count, block_rows, head_count, DH)
    keys_home = triple[:, model_width : 2 * model_width].reshape(
        item_count, block_rows, model_width
    )
    values_home = triple[:, 2 * model_width :].reshape(item_count, block_rows, model_width)
    all_keys, all_values = in_one_piece((keys_home, values_home), "blk", 1, 0)

    def self_scores(keys_full):
        raw = (
            jnp.einsum(
                "bqhd,bkhd->bhqk",
                queries,
                keys_full.reshape(item_count, full_rows, head_count, DH),
                preferred_element_type=jnp.float32,
            )
            * score_scale
        )
        return jnp.where(causal[None, None], raw, masked_value)

    scores = self_scores(all_keys)
    highest = jnp.max(scores, axis=-1, keepdims=True)
    expon = jnp.exp(scores - highest)
    totals = jnp.sum(expon, axis=-1, keepdims=True)
    log_total = highest + jnp.log(totals)
    self_probs = narrow(expon / totals)
    attended = jnp.einsum(
        "bhqk,bkhd->bqhd",
        self_probs,
        all_values.reshape(item_count, full_rows, head_count, DH),
        preferred_element_type=jnp.float32,
    )
    attended = narrow(attended.reshape(tokens, model_width))
    after_self = inputs + matmul(attended, output_weight)
    normed_two, pull_two = jax.vjp(layer_norm, after_self, norm_gain[1], norm_shift[1])
    hidden_two = narrow(normed_two)
    cross_queries = narrow(matmul(hidden_two, query_weight)).reshape(
        item_count, block_rows, head_count, DH
    )
    memory = narrow(matmul(text_states, memory_weight))
    memory_keys = memory[:, :model_width].reshape(text_rows, head_count, DH)
    memory_values = memory[:, model_width:].reshape(text_rows, head_count, DH)
    allowed = (text_segment[None, :] == item_segment[:, None])[:, None, None, :]
    cross_raw = (
        jnp.einsum("bqhd,thd->bhqt", cross_queries, memory_keys, preferred_element_type=jnp.float32)
        * score_scale
    )
    cross_weights = jax.nn.softmax(jnp.where(allowed, cross_raw, masked_value), axis=-1)
    cross_probs = narrow(cross_weights)
    cross_attended = jnp.einsum(
        "bhqt,thd->bqhd", cross_probs, memory_values, preferred_element_type=jnp.float32
    )
    cross_attended = narrow(cross_attended.reshape(tokens, model_width))
    after_cross = after_self + matmul(cross_attended, return_weight)
    normed_three, pull_three = jax.vjp(layer_norm, after_cross, norm_gain[2], norm_shift[2])
    hidden_three = narrow(normed_three)
    lifted = matmul(hidden_three, up_weight) + inner_bias
    activated_full, pull_gelu = jax.vjp(jax.nn.gelu, lifted)
    activated = narrow(activated_full)
    result = after_cross + matmul(activated, down_weight) + outer_bias
    layer_output = narrow(result).reshape(item_count, block_rows, model_width)
    grad_out = cotangent.astype(jnp.float32).reshape(tokens, model_width)
    outer_term = jnp.sum(grad_out, axis=0)
    grad_half = narrow(grad_out)
    down_term = dot_left(activated, grad_half)
    grad_act = narrow(dot_right(grad_half, down_weight))
    grad_lift = narrow(pull_gelu(grad_act.astype(jnp.float32))[0])
    inner_term = jnp.sum(grad_lift.astype(jnp.float32), axis=0)
    up_term = dot_left(hidden_three, grad_lift)
    back_three, gain_three, shift_three = pull_three(dot_right(grad_lift, up_weight))
    grad_cross = grad_out + back_three
    branch_two = narrow(grad_cross)
    return_term = dot_left(cross_attended, branch_two)
    grad_cross_att = narrow(dot_right(branch_two, return_weight)).reshape(
        item_count, block_rows, head_count, DH
    )
    grad_cross_w = jnp.einsum(
        "bqhd,thd->bhqt", grad_cross_att, memory_values, preferred_element_type=jnp.float32
    )
    grad_cross_s = narrow(
        cross_weights
        * (grad_cross_w - jnp.sum(cross_weights * grad_cross_w, axis=-1, keepdims=True))
    )
    grad_cross_q = narrow(
        score_scale
        * jnp.einsum(
            "bhqt,thd->bqhd", grad_cross_s, memory_keys, preferred_element_type=jnp.float32
        )
    ).reshape(tokens, model_width)
    memory_key_part = score_scale * jnp.einsum(
        "bhqt,bqhd->bthd", grad_cross_s, cross_queries, preferred_element_type=jnp.float32
    )
    memory_value_part = jnp.einsum(
        "bhqt,bqhd->bthd", cross_probs, grad_cross_att, preferred_element_type=jnp.float32
    )
    key_share, value_share = tuple(
        (
            part.astype(jnp.float32)
            for part in side_by_side(
                (
                    memory_key_part.reshape(item_count, text_rows, model_width).astype(
                        jnp.bfloat16
                    ),
                    memory_value_part.reshape(item_count, text_rows, model_width).astype(
                        jnp.bfloat16
                    ),
                ),
                "blk",
                1,
                0,
            )
        )
    )
    share_rows = text_rows // cycle_size
    grad_memory = narrow(jnp.concatenate([key_share, value_share], axis=-1))
    text_part = lax.dynamic_slice_in_dim(text_states, cycle_index * share_rows, share_rows, 0)
    memory_term = jnp.einsum(
        "tc,btm->cm", text_part, grad_memory, preferred_element_type=jnp.float32
    )
    text_share_term = jnp.einsum(
        "btm,cm->tc", grad_memory, memory_weight, preferred_element_type=jnp.float32
    )
    text_term = lax.dynamic_update_slice_in_dim(
        jnp.zeros((text_rows, model_width), jnp.float32),
        text_share_term,
        cycle_index * share_rows,
        0,
    )
    query_term = dot_left(hidden_two, grad_cross_q)
    back_two, gain_two, shift_two = pull_two(dot_right(grad_cross_q, query_weight))
    grad_self = grad_cross + back_two
    branch_one = narrow(grad_self)
    output_term = dot_left(attended, branch_one)
    grad_att = narrow(dot_right(branch_one, output_weight)).reshape(
        item_count, block_rows, head_count, DH
    )
    keys_back, values_back = (all_keys, all_values)
    probs = jnp.exp(self_scores(keys_back) - log_total)
    grad_probs = jnp.einsum(
        "bqhd,bkhd->bhqk",
        grad_att,
        values_back.reshape(item_count, full_rows, head_count, DH),
        preferred_element_type=jnp.float32,
    )
    row_dots = jnp.sum(probs * grad_probs, axis=-1, keepdims=True)
    grad_scores = narrow(probs * (grad_probs - row_dots))
    grad_queries = narrow(
        score_scale
        * jnp.einsum(
            "bhqk,bkhd->bqhd",
            grad_scores,
            keys_back.reshape(item_count, full_rows, head_count, DH),
            preferred_element_type=jnp.float32,
        )
    )
    key_part = score_scale * jnp.einsum(
        "bhqk,bqhd->bkhd", grad_scores, queries, preferred_element_type=jnp.float32
    )
    value_part = jnp.einsum(
        "bhqk,bqhd->bkhd", narrow(probs), grad_att, preferred_element_type=jnp.float32
    )
    key_home_grad, value_home_grad = tuple(
        (
            part.astype(jnp.float32)
            for part in side_by_side(
                (
                    key_part.reshape(item_count, full_rows, model_width).astype(jnp.bfloat16),
                    value_part.reshape(item_count, full_rows, model_width).astype(jnp.bfloat16),
                ),
                "blk",
                1,
                0,
            )
        )
    )
    grad_triple = jnp.concatenate(
        [
            grad_queries.reshape(tokens, model_width),
            narrow(key_home_grad).reshape(tokens, model_width),
            narrow(value_home_grad).reshape(tokens, model_width),
        ],
        axis=1,
    )
    triple_term = dot_left(hidden_one, grad_triple)
    back_one, gain_one, shift_one = pull_one(dot_right(grad_triple, triple_weight))
    input_grad = (grad_self + back_one).reshape(item_count, block_rows, model_width)
    gain_term = jnp.stack([gain_one, gain_two, gain_three])
    shift_term = jnp.stack([shift_one, shift_two, shift_three])
    (
        text_section,
        gain_section,
        shift_section,
        triple_section,
        output_section,
        query_section,
        memory_section,
        return_section,
        up_section,
        inner_section,
        down_section,
        outer_section,
    ) = (
        *tuple(
            (
                part.astype(jnp.float32)
                for part in side_by_side(
                    (
                        text_term.astype(jnp.bfloat16),
                        gain_term.astype(jnp.bfloat16),
                        shift_term.astype(jnp.bfloat16),
                    ),
                    "dp",
                    1,
                    0,
                )
            )
        ),
        *tuple(
            (
                part.astype(jnp.float32)
                for part in side_by_side(
                    (
                        triple_term.astype(jnp.bfloat16),
                        output_term.astype(jnp.bfloat16),
                        query_term.astype(jnp.bfloat16),
                        memory_term.astype(jnp.bfloat16),
                        return_term.astype(jnp.bfloat16),
                        up_term.astype(jnp.bfloat16),
                    ),
                    "dp",
                    0,
                    1,
                )
            )
        ),
        *tuple(
            (
                part.astype(jnp.float32)
                for part in sent_together(
                    (inner_term.astype(jnp.bfloat16), down_term.astype(jnp.bfloat16)), "dp", 0, 1
                )
            )
        ),
        lax.psum_scatter(
            outer_term.astype(jnp.bfloat16), "dp", scatter_dimension=0, tiled=True
        ).astype(jnp.float32),
    )
    (
        text_grad,
        gain_grad,
        shift_grad,
        triple_grad,
        output_grad,
        query_grad,
        memory_grad,
        return_grad,
        up_grad,
        inner_grad,
        down_grad,
        outer_grad,
    ) = tuple(
        (
            part.astype(jnp.float32)
            for part in one_scatter(
                (
                    text_section.astype(jnp.bfloat16),
                    gain_section.astype(jnp.bfloat16),
                    shift_section.astype(jnp.bfloat16),
                    triple_section.astype(jnp.bfloat16),
                    output_section.astype(jnp.bfloat16),
                    query_section.astype(jnp.bfloat16),
                    memory_section.astype(jnp.bfloat16),
                    return_section.astype(jnp.bfloat16),
                    up_section.astype(jnp.bfloat16),
                    inner_section.astype(jnp.bfloat16),
                    down_section.astype(jnp.bfloat16),
                    outer_section.astype(jnp.bfloat16),
                ),
                "blk",
                (1, 1, 1, 0, 0, 0, 0, 0, 0, 0, 0, 0),
            )
        )
    )
    return (
        layer_output,
        input_grad,
        text_grad,
        gain_grad,
        shift_grad,
        triple_grad,
        output_grad,
        query_grad,
        memory_grad,
        return_grad,
        up_grad,
        inner_grad,
        down_grad,
        outer_grad,
    )


def solution(mesh):
    placed = (
        P("dp", "blk", None),
        P(),
        P(),
        P("dp"),
        P(),
        P(),
        P(),
        P(),
        P(),
        P(),
        P(),
        P(),
        P(),
        P(),
        P(),
        P("dp", "blk", None),
    )
    return jax.shard_map(
        local,
        mesh=mesh,
        in_specs=placed,
        out_specs=(
            P("dp", "blk", None),
            P("dp", "blk", None),
            P(None, ("dp", "blk")),
            P(None, ("dp", "blk")),
            P(None, ("dp", "blk")),
            P(("dp", "blk"), None),
            P(("dp", "blk"), None),
            P(("dp", "blk"), None),
            P(("dp", "blk"), None),
            P(("dp", "blk"), None),
            P(("dp", "blk"), None),
            P(("dp", "blk")),
            P(("dp", "blk"), None),
            P(("dp", "blk")),
        ),
        check_vma=False,
    )
```

profile of v0, /device:TPU:0, one launch (start us, length us, event | category | flops | bytes accessed | tf_op | source)
XLA Modules:
  0.0 1032.0 jit_solution(16090967294679910832)
XLA Ops:
  14.2 4.8 convolution_convert_fusion.2
  28.8 102.9 %all-gather.2.cloned.1.call-done = bf16[4,1024,1024]{2,1,0:T(8,128)(2,1)} async-done(((bf16[4,128,1024]{2,1,0:T(8,128)(2,1)}), bf16[4,1024,1024]{2,1,0:T(8,128)(2,1)}) %all-gather.2.cloned.1.call-update) | async-done | bytes 8388624 | tf_op jit(solution)/shard_map/all_gather | solution.py:18
  131.6 6.0 fusion.87
  137.6 6.3 copy.137
  143.9 6.2 copy.135
  150.1 4.8 fusion.7
  155.0 4.3 fusion.1
  160.7 7.2 fusion.34
  178.2 3.9 fusion.95
  187.5 6.0 convolution_add_fusion
  193.5 9.5 fusion.99
  203.0 3.2 multiply_reduce_fusion.1
  214.2 3.0 convolution_convert_fusion.8
  232.0 12.6 %fusion.18 = bf16[2,16,64,1024]{3,2,1,0:T(8,128)(2,1)} fusion(bf16[2,128,16,64]{1,3,2,0:T(8,128)(2,1)} %copy.151, f32[2,16,128]{2,1,0:T(8,128)S(1)} %log_add_fusion, f32[2,16,128,1024]{3,2,1,0:T(8,128)} %copy-done.2, pred[128,1024]{1,0:T(8,128)(4,1)S(1)} %iota_compare_fusion), kind=kOutput, calls=%fused_computation.38 | convolution fusion | flops 555745280 | bytes 21643264 | tf_op jit(solution)/shard_map/bhqk,bqhd->bkhd/dot_general | solution.py:283
  244.6 13.1 %multiply_reduce_fusion = (f32[2,16,128]{2,1,0:T(8,128)S(1)}, f32[2,16,128,1024]{3,2,1,0:T(8,128)}) fusion(f32[2,16,128]{2,1,0:T(8,128)S(1)} %log_add_fusion, f32[2,16,128,1024]{3,2,1,0:T(8,128)} %copy-done.2, pred[128,1024]{1,0:T(8,128)(4,1)S(1)} %iota_compare_fusion, bf16[2,128,16,64]{1,3,2,0:T(8,128)(2,1)S(1)} %copy-done.30, ...), kind=kOutput, calls=%fused_computation.2 | convolution fusion | flops 557838336 | bytes 38436864 | tf_op jit(solution)/shard_map/bqhd,bkhd->bhqk/dot_general | solution.py:263
  261.8 6.6 copy.156
  268.4 12.1 %multiply_convert_fusion = bf16[2,16,128,1024]{3,2,1,0:T(8,128)(2,1)S(1)} fusion(f32[2,16,128,1024]{3,2,1,0:T(8,128)} %get-tuple-element.114, f32[2,16,128]{2,1,0:T(8,128)S(1)} %get-tuple-element.113, f32[2,16,128]{2,1,0:T(8,128)S(1)} %log_add_fusion, f32[2,16,128,1024]{3,2,1,0:T(8,128)} %copy-done.2, pred[128,1024]{1,0:T(8,128)(4,1)S(1)} %iota_compare_fusion), kind=kLoop, calls=%fused_computation.1 | loop fusion | flops 25165824 | bytes 42106880 | tf_op jit(solution)/shard_map/convert_element_type | solution.py:75
  280.5 3.7 multiply_convert_fusion.1
  285.0 6.2 copy.155
  291.2 7.5 pad_maximum_fusion.1
  299.8 8.0 convolution_convert_fusion
  307.7 9.4 pad_maximum_fusion
  320.2 3.1 convolution_convert_fusion.5
  323.3 4.1 copy.182
  331.4 4.0 copy.181
  337.5 3.9 copy.180
  341.4 7.7 fusion.31
  351.1 3.5 fusion.100
  355.6 109.3 %reduce-scatter.6.cloned.1.call-done = bf16[4,128,1024]{2,1,0:T(8,128)(2,1)} async-done(((bf16[4,1024,1024]{2,1,0:T(8,128)(2,1)}), bf16[4,128,1024]{2,1,0:T(8,128)(2,1)}) %reduce-scatter.6.cloned.1.call-update) | async-done | bytes 1048592 | tf_op jit(solution)/shard_map/reduce_scatter | solution.py:32
  468.3 5.2 fusion.84
  475.0 3.7 concatenate.34
  478.7 6.2 convert_dynamic-update-slice_fusion.1
  488.9 4.3 convert_dynamic-update-slice_fusion.2
  493.2 3.4 constant_dynamic-update-slice_fusion
  496.7 5.8 convert_dynamic-update-slice_fusion
  504.8 30.4 %all-reduce.2 = bf16[1024]{0:T(1024)(128)(2,1)S(1)} all-reduce(bf16[1024]{0:T(1024)(128)(2,1)S(1)} %reduce_sum.307), channel_id=7, replica_groups=mesh['dp'=16,'blk'=8] {'dp'}, use_global_device_ids=true, to_apply=%region_32.33.clone | all-reduce | flops 1024 | bytes 4096
  535.9 29.1 %reduce-scatter.12.cloned.1.call-done = bf16[256,1025]{0,1:T(8,128)(2,1)} async-done(((bf16[4096,1025]{0,1:T(8,128)(2,1)}), bf16[256,1025]{0,1:T(8,128)(2,1)}) %reduce-scatter.12.cloned.1.call-update) | async-done | bytes 524816 | tf_op jit(solution)/shard_map/reduce_scatter | solution.py:41
  568.0 58.7 %reduce-scatter.8.cloned.1.call-done = bf16[134,64]{0,1:T(8,128)(2,1)} async-done(((bf16[134,1024]{0,1:T(8,128)(2,1)}), bf16[134,64]{0,1:T(8,128)(2,1)}) %reduce-scatter.8.cloned.1.call-update) | async-done | bytes 17168 | tf_op jit(solution)/shard_map/reduce_scatter | solution.py:32
  632.6 262.0 %reduce-scatter.10.cloned.1.call-done = bf16[64,12288]{1,0:T(8,128)(2,1)} async-done(((bf16[1024,12288]{1,0:T(8,128)(2,1)}), bf16[64,12288]{1,0:T(8,128)(2,1)}) %reduce-scatter.10.cloned.1.call-update) | async-done | bytes 1572880 | tf_op jit(solution)/shard_map/reduce_scatter | solution.py:32
  900.3 3.7 dynamic-update-slice.3
  908.2 3.1 dynamic-update-slice.6
  913.4 4.3 dynamic-update-slice.8
  919.2 4.0 dynamic-update-slice.10
  924.5 3.0 pad.4
  927.5 3.9 reshape.384
  931.5 8.3 fusion.26
  941.2 63.1 %reduce-scatter.14.cloned.1.call-done = bf16[1040,128]{1,0:T(8,128)(2,1)} async-done(((bf16[8320,128]{1,0:T(8,128)(2,1)}), bf16[1040,128]{1,0:T(8,128)(2,1)}) %reduce-scatter.14.cloned.1.call-update) | async-done | bytes 266256 | tf_op jit(solution)/shard_map/reduce_scatter | solution.py:59
  1016.5 6.8 slice.94
  (332 shorter events, 123.0 us)
Async XLA Ops:
  7.2 165.4 %copy-start = (bf16[1024,1024]{1,0:T(8,128)(2,1)S(1)}, bf16[1024,1024]{1,0:T(8,128)(2,1)}, u32[]{:S(2)}) copy-start(bf16[1024,1024]{1,0:T(8,128)(2,1)} %param.24) | copy-start | bytes 6291460
  7.2 124.4 %all-gather.2.cloned.1.call-start = ((), (), s32[]{:S(2)}) async-start(), calls=%async_computation.5 | async-start | bytes 9437184 | tf_op jit(solution)/shard_map/all_gather | solution.py:18
  20.2 329.6 %all-reduce.5.cloned.1.call-start = ((), (), s32[]{:S(2)}) async-start(), calls=%async_computation.11 | async-start | bytes 2097152
  20.3 7.7 copy-start.81
  20.3 7.7 copy-start.82
  27.9 122.2 %copy-start.18 = (bf16[2,128,16,64]{1,3,2,0:T(8,128)(2,1)}, bf16[2,128,16,64]{1,3,2,0:T(8,128)(2,1)S(1)}, u32[]{:S(2)}) copy-start(bf16[2,128,16,64]{1,3,2,0:T(8,128)(2,1)S(1)} %copy.138) | copy-start | bytes 1572868
  155.0 5.8 copy-start.2
  160.7 7.8 copy-start.4
  187.1 19.1 %copy-start.9 = (f32[256,1024]{1,0:T(8,128)}, f32[256,1024]{1,0:T(8,128)S(1)}, u32[]{:S(2)}) copy-start(f32[256,1024]{1,0:T(8,128)S(1)} %get-tuple-element.108) | copy-start | bytes 3145732
  187.1 19.1 %copy-start.67 = (f32[256]{0:T(256)}, f32[256]{0:T(256)S(1)}, u32[]{:S(2)}) copy-start(f32[256]{0:T(256)S(1)} %broadcast_multiply_fusion) | copy-start | bytes 3076
  187.4 18.8 %copy-start.72 = (f32[256]{0:T(256)}, f32[256]{0:T(256)S(1)}, u32[]{:S(2)}) copy-start(f32[256]{0:T(256)S(1)} %fusion.69) | copy-start | bytes 3076
  187.4 6.0 copy-start.22
  187.5 15.5 %slice-start = ((s8[8388608]{0:T(1024)(128)(4,1)}), s8[4194304]{0:T(1024)(128)(4,1)S(1)}, s32[]{:S(2)}) async-start(s8[8388608]{0:T(1024)(128)(4,1)} %bitcast.241), calls=%async_computation.12 | async-start | bytes 8388608
  193.5 9.5 copy-start.87
  193.5 9.5 slice-start.1
  226.8 108.6 %copy-start.6 = (f32[256,1024]{1,0:T(8,128)}, f32[256,1024]{1,0:T(8,128)S(1)}, u32[]{:S(2)}) copy-start(f32[256,1024]{1,0:T(8,128)S(1)} %add_add_fusion.4) | copy-start | bytes 3145732
  231.9 12.6 %copy-start.8 = (bf16[2,1024,1024]{1,2,0:T(8,128)(2,1)S(1)}, bf16[2,1024,1024]{1,2,0:T(8,128)(2,1)}, u32[]{:S(2)}) copy-start(bf16[2,1024,1024]{1,2,0:T(8,128)(2,1)} %copy.135) | copy-start | bytes 12582916
  231.9 12.6 %copy-start.30 = (bf16[2,128,16,64]{1,3,2,0:T(8,128)(2,1)S(1)}, bf16[2,128,16,64]{1,3,2,0:T(8,128)(2,1)}, u32[]{:S(2)}) copy-start(bf16[2,128,16,64]{1,3,2,0:T(8,128)(2,1)} %copy.151) | copy-start | bytes 1572868
  244.6 13.1 %copy-start.34 = (bf16[2,16,64,128]{3,2,1,0:T(8,128)(2,1)S(1)}, bf16[2,16,64,128]{3,2,1,0:T(8,128)(2,1)}, u32[]{:S(2)}) copy-start(bf16[2,16,64,128]{3,2,1,0:T(8,128)(2,1)} %convolution_convert_fusion.8) | copy-start | bytes 1572868
  261.7 203.2 %reduce-scatter.6.cloned.1.call-start = ((), (), s32[]{:S(2)}) async-start(), calls=%async_computation.6 | async-start | bytes 9437184 | tf_op jit(solution)/shard_map/reduce_scatter | solution.py:32
  268.4 12.1 %copy-start.19 = (bf16[2,128,16,64]{1,3,2,0:T(8,128)(2,1)S(1)}, bf16[2,128,16,64]{1,3,2,0:T(8,128)(2,1)}, u32[]{:S(2)}) copy-start(bf16[2,128,16,64]{1,3,2,0:T(8,128)(2,1)} %copy-done.18) | copy-start | bytes 1572868
  298.8 266.3 %reduce-scatter.12.cloned.1.call-start = ((), (), s32[]{:S(2)}) async-start(), calls=%async_computation.9 | async-start | bytes 8982528 | tf_op jit(solution)/shard_map/reduce_scatter | solution.py:41
  317.2 309.6 %reduce-scatter.8.cloned.1.call-start = ((), (), s32[]{:S(2)}) async-start(), calls=%async_computation.7 | async-start | bytes 557056 | tf_op jit(solution)/shard_map/reduce_scatter | solution.py:32
  319.0 10.2 copy-start.33
  319.1 10.2 copy-start.48
  319.1 10.1 copy-start.52
  319.1 10.1 copy-start.59
  319.1 10.1 copy-start.62
  327.4 8.0 copy-start.21
  349.7 118.5 %copy-start.40 = (bf16[128,8,2,128]{3,1,2,0:T(8,128)(2,1)}, bf16[128,8,2,128]{3,1,2,0:T(8,128)(2,1)S(1)}, u32[]{:S(2)}) copy-start(bf16[128,8,2,128]{3,1,2,0:T(8,128)(2,1)S(1)} %copy.260) | copy-start | bytes 1572868
  351.1 117.1 %copy-start.5 = (bf16[2,128,1024]{2,1,0:T(8,128)(2,1)S(1)}, bf16[2,128,1024]{2,1,0:T(8,128)(2,1)}, u32[]{:S(2)}) copy-start(bf16[2,128,1024]{2,1,0:T(8,128)(2,1)} %param.16) | copy-start | bytes 1572868
  351.1 117.1 %copy-start.45 = (f32[1,1024]{1,0:T(1,128)S(1)}, f32[1,1024]{1,0:T(1,128)}, u32[]{:S(2)}) copy-start(f32[1,1024]{1,0:T(1,128)} %copy-done.44) | copy-start | bytes 12292
  351.1 117.1 %copy-start.54 = (f32[256]{0:T(256)S(1)}, f32[256]{0:T(256)}, u32[]{:S(2)}) copy-start(f32[256]{0:T(256)} %copy-done.53) | copy-start | bytes 3076
  468.2 6.7 copy-start.36
  468.2 6.7 copy-start.37
  468.2 6.7 copy-start.38
  478.7 6.2 copy-start.16
  488.9 7.8 copy-start.10
  488.9 7.8 copy-start.50
  488.9 7.8 copy-start.68
  488.9 7.8 copy-start.73
  488.9 7.8 copy-start.76
  493.2 401.5 %reduce-scatter.10.cloned.1.call-start = ((), (), s32[]{:S(2)}) async-start(), calls=%async_computation.8 | async-start | bytes 26738688 | tf_op jit(solution)/shard_map/reduce_scatter | solution.py:32
  502.5 501.9 %reduce-scatter.14.cloned.1.call-start = ((), (), s32[]{:S(2)}) async-start(), calls=%async_computation.10 | async-start | bytes 2396160 | tf_op jit(solution)/shard_map/reduce_scatter | solution.py:59
  931.4 8.4 copy-start.74
  931.5 8.4 copy-start.7
  931.5 8.4 copy-start.29
  939.8 84.9 %copy-start.1 = (bf16[1024,1024]{1,0:T(8,128)(2,1)S(1)}, bf16[1024,1024]{1,0:T(8,128)(2,1)}, u32[]{:S(2)}) copy-start(bf16[1024,1024]{1,0:T(8,128)(2,1)} %param.24) | copy-start | bytes 6291460
  (49 other events, 126.8 us)
Sparse Core Ops, SparseCore 0:
  20.3 111.2 all-gather.1
  261.8 86.5 all-reduce.4
  352.3 112.5 reduce-scatter.5
  467.2 97.8 reduce-scatter.11
  567.3 59.4 reduce-scatter.7
  629.2 265.4 reduce-scatter.9
  931.5 72.7 reduce-scatter.13
where the time goes:
time: 1040 us; the launch traced here: 1030 us
  waiting for transfers between devices  625 us (60%)
  local copies, waits for them, and re-layouts  156 us (15%)
  matrix products  146 us (14%)
  other arithmetic  56.4 us (5%)
  blocking collectives  30.4 us (3%)
  between operations  17.3 us (2%)
    reduce_scatter x3, waiting for transfers between devices, side_by_side(): lax.psum_scatter(both, axis, scatter_dimension=dim, tiled=True)  430 us
    all_gather x1, waiting for transfers between devices, in_one_piece(): result, at, done = (lax.all_gather(both, axis, axis=dim, tiled=True), 0, [])  103 us
    reduce_scatter x1, waiting for transfers between devices, one_scatter(): lax.psum_scatter(lines, axis, tiled=True).reshape(-1)  63.1 us
    unnamed x199, local copies, waits for them, and re-layouts  45.5 us
    unnamed x1, blocking collectives  30.4 us
    reduce_scatter x1, waiting for transfers between devices, sent_together(): result = lax.psum_scatter(both, axis, scatter_dimension=dim, tiled=True)  29.1 us
    dot_general x6, matrix products, dot_left(): lax.dot_general(left, right, (((0,), (0,)), ((), ())), preferred_element_...  27.3 us
    dot_general x7, matrix products, matmul(): return jnp.dot(left, right, preferred_element_type=jnp.float32)  27 us
  transfers between devices with their start and end apart: 7, of which 6 were waited for; matrix products, arithmetic and copies ran while one was open for 15% of the time, Pallas kernels for 0%

commit v1 on v0

v1 whole, which is shorter than its diff:
```python
import functools

import jax
import jax.numpy as jnp
from jax import lax
from jax.experimental import pallas as pl
from jax.experimental.pallas import tpu as pltpu
from jax.sharding import Mesh, PartitionSpec as P

DH = 64
EPS = 1e-05
SCALE = 0.125
MASKED = -1e30
BF = jnp.bfloat16
F32 = jnp.float32
MIB = 1 << 20

BLK = ("x", "yh")
ALL = ("z", "yl", "c", "x", "yh")


def dot(a, b, ca=1, cb=0):
    return lax.dot_general(a, b, (((ca,), (cb,)), ((), ())), preferred_element_type=F32)


def cost(flops, nbytes, trans=0):
    return pl.CostEstimate(flops=int(flops), bytes_accessed=int(nbytes), transcendentals=int(trans))


def params(mib):
    return pltpu.CompilerParams(vmem_limit_bytes=mib * MIB)


SMEM = pl.BlockSpec(memory_space=pltpu.SMEM)


def whole(shape):
    return pl.BlockSpec(shape, lambda *_: (0,) * len(shape))


def normalise(v):
    mean = jnp.mean(v, axis=-1, keepdims=True)
    centred = v - mean
    var = jnp.mean(centred * centred, axis=-1, keepdims=True)
    rstd = lax.rsqrt(var + EPS)
    return centred * rstd, rstd


def norm_back(dy, xhat, rstd, gain):
    dx = dy * gain
    m1 = jnp.mean(dx, axis=-1, keepdims=True)
    m2 = jnp.mean(dx * xhat, axis=-1, keepdims=True)
    back = rstd * (dx - m1 - xhat * m2)
    dgain = jnp.sum(dy * xhat, axis=0, keepdims=True)
    dshift = jnp.sum(dy, axis=0, keepdims=True)
    return back, dgain, dshift


def triple_body(x_ref, g_ref, s_ref, perm_ref, wq_ref, wk_ref, wv_ref, p_ref, hm_ref, ht_ref, h_scr):
    @pl.when(pl.program_id(0) == 0)
    def _():
        xhat, _ = normalise(x_ref[...].astype(F32))
        h = (xhat * g_ref[...] + s_ref[...]).astype(BF)
        h_scr[...] = h
        hp = dot(h, perm_ref[...]).astype(BF)
        half = hp.shape[1] // 2
        hm_ref[...] = hp[:, :half]
        ht_ref[...] = hp[:, half:]

    h = h_scr[...]
    for i, w in enumerate((wq_ref, wk_ref, wv_ref)):
        r = dot(h, w[...]).astype(BF)
        p_ref[0, :, i * 128 : (i + 1) * 128] = r[:, :128]
        p_ref[1, :, i * 128 : (i + 1) * 128] = r[:, 128:]


def triple_forward(x, gain, shift, perm, w):
    t, d = x.shape
    n = d // 256
    return pl.pallas_call(
        triple_body,
        grid=(n,),
        in_specs=[
            whole((t, d)),
            whole((1, d)),
            whole((1, d)),
            whole((d, d)),
            pl.BlockSpec((d, 256), lambda j: (0, j)),
            pl.BlockSpec((d, 256), lambda j: (0, n + j)),
            pl.BlockSpec((d, 256), lambda j: (0, 2 * n + j)),
        ],
        out_specs=[
            pl.BlockSpec((2, t, 384), lambda j: (j, 0, 0)),
            whole((t, d // 2)),
            whole((t, d // 2)),
        ],
        out_shape=[
            jax.ShapeDtypeStruct((d // 128, t, 384), BF),
            jax.ShapeDtypeStruct((t, d // 2), BF),
            jax.ShapeDtypeStruct((t, d // 2), BF),
        ],
        scratch_shapes=[pltpu.VMEM((t, d), BF)],
        compiler_params=params(32),
        cost_estimate=cost(2 * t * d * 4 * d, 10 * MIB),
        name="triple_forward",
    )(x, gain, shift, perm, w, w, w)


def head_lanes(shape, h):
    return (lax.broadcasted_iota(jnp.int32, shape, 1) // DH) == h


def masked_head(v, h):
    return jnp.where(head_lanes(v.shape, h), v, 0.0).astype(BF)


def probs_t(k, qh, qb):
    kv = 256 * (qb + 1)
    st = dot(k[:kv], qh, 1, 1)
    kpos = lax.broadcasted_iota(jnp.int32, (256, 256), 0)
    qpos = lax.broadcasted_iota(jnp.int32, (256, 256), 1)
    last = jnp.where(kpos <= qpos, st[kv - 256 :], MASKED)
    st = jnp.concatenate([st[: kv - 256], last], axis=0) if qb else last
    top = jnp.max(st, axis=0, keepdims=True)
    e = jnp.exp(st - top)
    return e * (1.0 / jnp.sum(e, axis=0, keepdims=True))


def attend_body(p_ref, o_ref):
    rows = p_ref.shape[0] * p_ref.shape[2]
    k = p_ref[:, 0, :, 128:256].reshape(rows, 128)
    v = p_ref[:, 0, :, 256:384].reshape(rows, 128)
    vt = v.T
    for qb in range(rows // 256):
        q = p_ref[2 * qb : 2 * qb + 2, 0, :, 0:128].reshape(256, 128).astype(F32) * SCALE
        kv = 256 * (qb + 1)
        parts = []
        for h in range(2):
            a = probs_t(k, masked_head(q, h), qb).astype(BF)
            parts.append(dot(vt[h * DH : (h + 1) * DH, :kv], a))
        o = jnp.concatenate(parts, axis=0).T.astype(BF)
        o_ref[2 * qb : 2 * qb + 2, 0] = o.reshape(2, 128, 128)


def attend(p):
    b, items, r, _ = p.shape
    return pl.pallas_call(
        attend_body,
        grid=(items,),
        in_specs=[pl.BlockSpec((b, 1, r, 384), lambda i: (0, i, 0, 0))],
        out_specs=pl.BlockSpec((b, 1, r, 128), lambda i: (0, i, 0, 0)),
        out_shape=jax.ShapeDtypeStruct((b, items, r, 128), BF),
        compiler_params=params(32),
        cost_estimate=cost(2 * items * 2 * 10 * 65536 * 128 * 2, 3 * MIB, 4 * 655360),
        name="attend",
    )(p)


def attend_back_body(p_ref, do_ref, dp_ref, dk_scr, dv_scr):
    rows = p_ref.shape[0] * p_ref.shape[2]
    blocks = p_ref.shape[0]
    k = p_ref[:, 0, :, 128:256].reshape(rows, 128)
    v = p_ref[:, 0, :, 256:384].reshape(rows, 128)
    kt = k.T
    dk_scr[...] = jnp.zeros_like(dk_scr)
    dv_scr[...] = jnp.zeros_like(dv_scr)
    for qb in range(rows // 256):
        q = p_ref[2 * qb : 2 * qb + 2, 0, :, 0:128].reshape(256, 128).astype(F32) * SCALE
        do = do_ref[2 * qb : 2 * qb + 2, 0].reshape(256, 128).astype(F32)
        kv = 256 * (qb + 1)
        parts = []
        for h in range(2):
            qh = masked_head(q, h)
            doh = masked_head(do, h)
            a = probs_t(k, qh, qb)
            da = dot(v[:kv], doh, 1, 1)
            dots = jnp.sum(a * da, axis=0, keepdims=True)
            ds = (a * (da - dots)).astype(BF)
            dv_scr[:kv] += dot(a.astype(BF), doh)
            dk_scr[:kv] += dot(ds, qh)
            parts.append(dot(kt[h * DH : (h + 1) * DH, :kv], ds))
        dq = (jnp.concatenate(parts, axis=0) * SCALE).T.astype(BF)
        dp_ref[2 * qb : 2 * qb + 2, 0, :, 0:128] = dq.reshape(2, 128, 128)
    dp_ref[:, 0, :, 128:256] = dk_scr[...].astype(BF).reshape(blocks, -1, 128)
    dp_ref[:, 0, :, 256:384] = dv_scr[...].astype(BF).reshape(blocks, -1, 128)


def attend_back(p, do):
    b, items, r, _ = p.shape
    return pl.pallas_call(
        attend_back_body,
        grid=(items,),
        in_specs=[
            pl.BlockSpec((b, 1, r, 384), lambda i: (0, i, 0, 0)),
            pl.BlockSpec((b, 1, r, 128), lambda i: (0, i, 0, 0)),
        ],
        out_specs=pl.BlockSpec((b, 1, r, 384), lambda i: (0, i, 0, 0)),
        out_shape=jax.ShapeDtypeStruct((b, items, r, 384), BF),
        scratch_shapes=[pltpu.VMEM((b * r, 128), F32), pltpu.VMEM((b * r, 128), F32)],
        compiler_params=params(40),
        cost_estimate=cost(2 * items * 5 * 10 * 65536 * 128 * 2, 5 * MIB, 4 * 655360),
        name="attend_back",
    )(p, do)


def stack_heads(v, items):
    r = v.shape[0] // items
    parts = []
    for i in range(items):
        for h in range(2):
            parts.append(masked_head(v[i * r : (i + 1) * r], h))
    return jnp.concatenate(parts, axis=0)


def unstack_heads(v, items):
    r = v.shape[0] // (2 * items)
    parts = []
    for i in range(items):
        first = v[(2 * i) * r : (2 * i + 1) * r]
        second = v[(2 * i + 1) * r : (2 * i + 2) * r]
        parts.append(jnp.where(head_lanes(first.shape, 0), first, second))
    return jnp.concatenate(parts, axis=0)


def cross_probs_t(mk, q4, allowed):
    st = jnp.where(allowed, dot(mk, q4, 1, 1), MASKED)
    top = jnp.max(st, axis=0, keepdims=True)
    e = jnp.exp(st - top)
    return e * (1.0 / jnp.sum(e, axis=0, keepdims=True))


def allowed_mask(tseg_ref, iseg_ref, items, r):
    seg = tseg_ref[...]
    return jnp.concatenate(
        [jnp.broadcast_to(seg == iseg_ref[i], (seg.shape[0], 2 * r)) for i in range(items)], axis=1
    )


def middle_body(
    iseg_ref, o_ref, x_ref, wo_ref, g_ref, s_ref, wq_ref, m_ref, tseg_ref, wr_ref, perm_ref,
    y1_ref, qc_ref, y2_ref, h3_ref, om_ref, ot_ref, h2m_ref, h2t_ref, ocm_ref, oct_ref, h3m_ref, h3t_ref,
    oc_scr,
):
    items = iseg_ref.shape[0]
    t, d = x_ref.shape
    r = t // items
    perm = perm_ref[...]

    def permuted(v, mine, theirs):
        vp = dot(v, perm).astype(BF)
        mine[...] = vp[:, : d // 2]
        theirs[...] = vp[:, d // 2 :]

    o = jnp.concatenate([o_ref[j] for j in range(o_ref.shape[0])], axis=1)
    permuted(o, om_ref, ot_ref)
    y1 = x_ref[...].astype(F32) + dot(o, wo_ref[...])
    y1_ref[...] = y1
    xhat, _ = normalise(y1)
    h2 = (xhat * g_ref[1:2] + s_ref[1:2]).astype(BF)
    permuted(h2, h2m_ref, h2t_ref)
    qc_ref[...] = dot(h2, wq_ref[...]).astype(BF)
    allowed = allowed_mask(tseg_ref, iseg_ref, items, r)
    for p in range(d // 128):
        at = slice(p * 128, (p + 1) * 128)
        q4 = stack_heads(qc_ref[:, at].astype(F32) * SCALE, items)
        a = cross_probs_t(m_ref[:, at], q4, allowed).astype(BF)
        o4 = dot(a, m_ref[:, d + p * 128 : d + (p + 1) * 128], 0, 0)
        oc_scr[:, at] = unstack_heads(o4, items).astype(BF)
    oc = oc_scr[...]
    permuted(oc, ocm_ref, oct_ref)
    y2 = y1 + dot(oc, wr_ref[...])
    y2_ref[...] = y2
    xhat, _ = normalise(y2)
    h3 = (xhat * g_ref[2:3] + s_ref[2:3]).astype(BF)
    h3_ref[...] = h3
    permuted(h3, h3m_ref, h3t_ref)


def middle(iseg, o, x, wo, gain, shift, wq, m, tseg, wr, perm):
    t, d = x.shape
    args = (iseg, o, x, wo, gain, shift, wq, m, tseg, wr, perm)
    half = jax.ShapeDtypeStruct((t, d // 2), BF)
    full = jax.ShapeDtypeStruct((t, d), BF)
    wide = jax.ShapeDtypeStruct((t, d), F32)
    outs = [wide, full, wide, full] + [half] * 8
    return pl.pallas_call(
        middle_body,
        in_specs=[SMEM] + [pl.BlockSpec(memory_space=pltpu.VMEM)] * 10,
        out_specs=[pl.BlockSpec(memory_space=pltpu.VMEM)] * len(outs),
        out_shape=outs,
        scratch_shapes=[pltpu.VMEM((t, d), BF)],
        compiler_params=params(40),
        cost_estimate=cost(2 * t * d * d * 7, 14 * MIB, 16 * 128 * t),
        name="middle",
    )(*args)


def mlp_body(
    c_ref, h3_ref, up_ref, ib_ref, down_ref, ob_ref, r_ref, y2_ref, g_ref,
    gm_ref, gt_ref, du_ref, inner_ref, out_ref, dy2_ref, dgain_ref, dshift_ref, outer_ref,
    y_scr, dh_scr,
):
    step = pl.program_id(0)

    @pl.when(step == 0)
    def _():
        y_scr[...] = jnp.zeros_like(y_scr)
        dh_scr[...] = jnp.zeros_like(dh_scr)

    up = up_ref[...]
    down = down_ref[...]
    cotangent = r_ref[...]
    u = dot(h3_ref[...], up) + ib_ref[...]
    dg = dot(cotangent, down, 1, 1).astype(BF).astype(F32)
    c0 = 0.7978845608028654
    c1 = 0.044715
    uu = u * u
    t = jnp.tanh(c0 * (u + c1 * (uu * u)))
    half = 0.5 * (1.0 + t)
    g = (u * half).astype(BF)
    slope = half + (0.5 * u) * (1.0 - t * t) * (c0 * (1.0 + (3.0 * c1) * uu))
    du = (slope * dg).astype(BF)
    du_ref[...] = du
    inner_ref[...] = jnp.sum(du.astype(F32), axis=0, keepdims=True)
    w = gm_ref.shape[1]
    first = c_ref[0] == 0

    @pl.when(first)
    def _():
        gm_ref[...] = g[:, :w]
        gt_ref[...] = g[:, w:]

    @pl.when(jnp.logical_not(first))
    def _():
        gm_ref[...] = g[:, w:]
        gt_ref[...] = g[:, :w]

    y_scr[...] += dot(g, down)
    dh_scr[...] += dot(du, up, 1, 1)

    @pl.when(step == pl.num_programs(0) - 1)
    def _():
        y2 = y2_ref[...]
        out_ref[...] = (y2 + y_scr[...] + ob_ref[...]).astype(BF)
        xhat, rstd = normalise(y2)
        back, dgain, dshift = norm_back(dh_scr[...], xhat, rstd, g_ref[2:3])
        cot = cotangent.astype(F32)
        dy2_ref[...] = cot + back
        dgain_ref[...] = dgain
        dshift_ref[...] = dshift
        outer_ref[...] = jnp.sum(cot, axis=0, keepdims=True)


def mlp(c, h3, up, ib, down, ob, cot, y2, gain):
    t, d = h3.shape
    ff = up.shape[1]
    tile = 512
    n = ff // tile
    row = jax.ShapeDtypeStruct((1, d), F32)
    return pl.pallas_call(
        mlp_body,
        grid=(n,),
        in_specs=[
            SMEM,
            whole((t, d)),
            pl.BlockSpec((d, tile), lambda i: (0, i)),
            pl.BlockSpec((1, tile), lambda i: (0, i)),
            pl.BlockSpec((tile, d), lambda i: (i, 0)),
            whole((1, d)),
            whole((t, d)),
            whole((t, d)),
            whole((3, d)),
        ],
        out_specs=[
            pl.BlockSpec((t, tile // 2), lambda i: (0, i)),
            pl.BlockSpec((t, tile // 2), lambda i: (0, i)),
            pl.BlockSpec((t, tile), lambda i: (0, i)),
            pl.BlockSpec((1, tile), lambda i: (0, i)),
            whole((t, d)),
            whole((t, d)),
            whole((1, d)),
            whole((1, d)),
            whole((1, d)),
        ],
        out_shape=[
            jax.ShapeDtypeStruct((t, ff // 2), BF),
            jax.ShapeDtypeStruct((t, ff // 2), BF),
            jax.ShapeDtypeStruct((t, ff), BF),
            jax.ShapeDtypeStruct((1, ff), F32),
            jax.ShapeDtypeStruct((t, d), BF),
            jax.ShapeDtypeStruct((t, d), F32),
            row,
            row,
            row,
        ],
        scratch_shapes=[pltpu.VMEM((t, d), F32), pltpu.VMEM((t, d), F32)],
        compiler_params=params(40),
        cost_estimate=cost(2 * t * d * ff * 4, 24 * MIB, t * ff),
        name="mlp",
    )(c, h3, up, ib, down, ob, cot, y2, gain)


def middle_back_body(
    iseg_ref, dy2_ref, wr_ref, qc_ref, m_ref, tseg_ref, wq_ref, y1_ref, g_ref, wo_ref,
    b2_ref, dqc_ref, b1_ref, dy1_ref, do_ref, dm_ref, dgain_ref, dshift_ref,
    doc_scr,
):
    items = iseg_ref.shape[0]
    t, d = dy2_ref.shape
    r = t // items
    dy2 = dy2_ref[...]
    b2 = dy2.astype(BF)
    b2_ref[...] = b2
    doc_scr[...] = dot(b2, wr_ref[...], 1, 1).astype(BF)
    allowed = allowed_mask(tseg_ref, iseg_ref, items, r)
    for p in range(d // 128):
        at = slice(p * 128, (p + 1) * 128)
        av = slice(d + p * 128, d + (p + 1) * 128)
        mk = m_ref[:, at]
        q4 = stack_heads(qc_ref[:, at].astype(F32) * SCALE, items)
        do4 = stack_heads(doc_scr[:, at].astype(F32), items)
        a = cross_probs_t(mk, q4, allowed)
        da = dot(m_ref[:, av], do4, 1, 1)
        dots = jnp.sum(a * da, axis=0, keepdims=True)
        ds = (a * (da - dots)).astype(BF)
        dm_ref[:, at] = dot(ds, q4)
        dm_ref[:, av] = dot(a.astype(BF), do4)
        dqc_ref[:, at] = (unstack_heads(dot(ds, mk, 0, 0), items) * SCALE).astype(BF)
    xhat, rstd = normalise(y1_ref[...])
    dh2 = dot(dqc_ref[...], wq_ref[...], 1, 1)
    back, dgain, dshift = norm_back(dh2, xhat, rstd, g_ref[1:2])
    dgain_ref[...] = dgain
    dshift_ref[...] = dshift
    dy1 = dy2 + back
    dy1_ref[...] = dy1
    b1 = dy1.astype(BF)
    b1_ref[...] = b1
    do = dot(b1, wo_ref[...], 1, 1).astype(BF)
    for j in range(do_ref.shape[0]):
        do_ref[j] = do[:, j * 128 : (j + 1) * 128]


def middle_back(iseg, dy2, wr, qc, m, tseg, wq, y1, gain, wo):
    t, d = dy2.shape
    args = (iseg, dy2, wr, qc, m, tseg, wq, y1, gain, wo)
    full = jax.ShapeDtypeStruct((t, d), BF)
    row = jax.ShapeDtypeStruct((1, d), F32)
    outs = [
        full, full, full, jax.ShapeDtypeStruct((t, d), F32), jax.ShapeDtypeStruct((d // 128, t, 128), BF),
        jax.ShapeDtypeStruct(m.shape, F32), row, row,
    ]
    return pl.pallas_call(
        middle_back_body,
        in_specs=[SMEM] + [pl.BlockSpec(memory_space=pltpu.VMEM)] * 9,
        out_specs=[pl.BlockSpec(memory_space=pltpu.VMEM)] * len(outs),
        out_shape=outs,
        scratch_shapes=[pltpu.VMEM((t, d), BF)],
        compiler_params=params(40),
        cost_estimate=cost(2 * t * d * d * 4, 14 * MIB, 16 * 128 * t),
        name="middle_back",
    )(*args)


def triple_back_body(dp_ref, wq_ref, wk_ref, wv_ref, x_ref, g_ref, dy1_ref, out_ref, dgain_ref, dshift_ref, flat_ref, acc):
    step = pl.program_id(0)
    n = pl.num_programs(0)

    @pl.when(step == 0)
    def _():
        acc[...] = jnp.zeros_like(acc)

    total = acc[...]
    for i, w in enumerate((wq_ref, wk_ref, wv_ref)):
        at = slice(i * 128, (i + 1) * 128)
        dp = jnp.concatenate([dp_ref[0, :, at], dp_ref[1, :, at]], axis=1)
        flat_ref[i] = dp
        total += dot(dp, w[...], 1, 1)
    acc[...] = total

    @pl.when(step == n - 1)
    def _():
        xhat, rstd = normalise(x_ref[...].astype(F32))
        back, dgain, dshift = norm_back(acc[...], xhat, rstd, g_ref[0:1])
        out_ref[...] = dy1_ref[...] + back
        dgain_ref[...] = dgain
        dshift_ref[...] = dshift


def triple_back(dp, w, x, gain, dy1):
    t, d = x.shape
    n = d // 256
    row = jax.ShapeDtypeStruct((1, d), F32)
    return pl.pallas_call(
        triple_back_body,
        grid=(n,),
        in_specs=[
            pl.BlockSpec((2, t, 384), lambda j: (j, 0, 0)),
            pl.BlockSpec((d, 256), lambda j: (0, j)),
            pl.BlockSpec((d, 256), lambda j: (0, n + j)),
            pl.BlockSpec((d, 256), lambda j: (0, 2 * n + j)),
            whole((t, d)),
            whole((3, d)),
            whole((t, d)),
        ],
        out_specs=[whole((t, d)), whole((1, d)), whole((1, d)), pl.BlockSpec((3, t, 256), lambda j: (0, 0, j))],
        out_shape=[
            jax.ShapeDtypeStruct((t, d), F32),
            row,
            row,
            jax.ShapeDtypeStruct((3, t, d), BF),
        ],
        scratch_shapes=[pltpu.VMEM((t, d), F32)],
        compiler_params=params(32),
        cost_estimate=cost(2 * t * d * 3 * d, 12 * MIB),
        name="triple_back",
    )(dp, w, w, w, x, gain, dy1)


def rows_grad_body(lm_ref, lp_ref, rm_ref, rp_ref, out_ref, lt_scr):
    t = lm_ref.shape[0]

    @pl.when(pl.program_id(0) == 0)
    def _():
        lt_scr[:, :t] = lm_ref[...].T
        lt_scr[:, t:] = lp_ref[...].T

    right = jnp.concatenate([rm_ref[...], rp_ref[...]], axis=0)
    out_ref[...] = dot(lt_scr[...], right).astype(BF)


def rows_grad(lm, lp, rm, rp, name):
    t, rows = lm.shape
    n = rm.shape[1]
    tile = 512
    return pl.pallas_call(
        rows_grad_body,
        grid=(n // tile,),
        in_specs=[
            whole((t, rows)),
            whole((t, rows)),
            pl.BlockSpec((t, tile), lambda j: (0, j)),
            pl.BlockSpec((t, tile), lambda j: (0, j)),
        ],
        out_specs=pl.BlockSpec((rows, tile), lambda j: (0, j)),
        out_shape=jax.ShapeDtypeStruct((rows, n), BF),
        scratch_shapes=[pltpu.VMEM((rows, 2 * t), BF)],
        compiler_params=params(32),
        cost_estimate=cost(2 * 2 * t * rows * n, 2 * (rows * n + 2 * t * n)),
        name=name,
    )(lm, lp, rm, rp)


def triple_grad_local(lm, lp, rm, rp):
    t, rows = lm.shape
    d = rm.shape[2]
    tile = 512
    per = d // tile
    return pl.pallas_call(
        rows_grad_body,
        grid=(3 * per,),
        in_specs=[
            whole((t, rows)),
            whole((t, rows)),
            pl.BlockSpec((None, t, tile), lambda j: (j // per, 0, j % per)),
            pl.BlockSpec((None, t, tile), lambda j: (j // per, 0, j % per)),
        ],
        out_specs=pl.BlockSpec((rows, tile), lambda j: (0, j)),
        out_shape=jax.ShapeDtypeStruct((rows, 3 * d), BF),
        scratch_shapes=[pltpu.VMEM((rows, 2 * t), BF)],
        compiler_params=params(32),
        cost_estimate=cost(2 * 2 * t * rows * 3 * d, 2 * (rows * 3 * d + 2 * t * 3 * d)),
        name="triple_grad_local",
    )(lm, lp, rm, rp)


def down_grad_body(gm_ref, gp_ref, rm_ref, rp_ref, out_ref):
    left = jnp.concatenate([gm_ref[...].T, gp_ref[...].T], axis=1)
    right = jnp.concatenate([rm_ref[...], rp_ref[...]], axis=0)
    out_ref[...] = dot(left, right).astype(BF).reshape(out_ref.shape)


def down_grad_local(gm, gp, rm, rp):
    t, d = rm.shape
    return pl.pallas_call(
        down_grad_body,
        grid=(4, 2),
        in_specs=[
            pl.BlockSpec((t, 256), lambda z, y: (0, 2 * z + y)),
            pl.BlockSpec((t, 256), lambda z, y: (0, 2 * z + y)),
            whole((t, d)),
            whole((t, d)),
        ],
        out_specs=pl.BlockSpec((1, 4, 2, 1, 32, d), lambda z, y: (z, 0, 0, y, 0, 0)),
        out_shape=jax.ShapeDtypeStruct((4, 4, 2, 2, 32, d), BF),
        compiler_params=params(32),
        cost_estimate=cost(2 * 2 * t * 2048 * d, 10 * MIB),
        name="down_grad_local",
    )(gm, gp, rm, rp)


RINGS = {"z": "z", "x": "x", "y": ("yl", "yh")}


def ring_place(axis):
    if axis == "y":
        return lax.axis_index("yh") * 2 + lax.axis_index("yl")
    return lax.axis_index(axis)


def ring_pairs(axis, step):
    if axis == "y":
        place = (0, 2, 1, 3)
        return [(place[i], place[(i + step) % 4]) for i in range(4)]
    return [(i, (i + step) % 4) for i in range(4)]


def ring_scatter(buf, axis, dim):
    me = ring_place(axis)

    def piece(k):
        return lax.dynamic_index_in_dim(buf, (me + k) % 4, dim, keepdims=False)

    got = [lax.ppermute(piece(k), RINGS[axis], ring_pairs(axis, k)) for k in (1, 3, 2)]
    total = piece(0).astype(F32)
    for g in got:
        total = total + g.astype(F32)
    return total


def scatter_all(buf, order):
    dims = ["z", "x", "y"]
    for i, axis in enumerate(order):
        total = ring_scatter(buf, axis, dims.index(axis))
        dims.remove(axis)
        buf = total.astype(BF) if i < 2 else total
    return buf


def to_partner(v):
    return lax.ppermute(v, "c", [(0, 1), (1, 0)])


def by_owner(v, rest):
    v = v.reshape(4, 2, 2, 4, 2, rest)
    return v.transpose(2, 0, 3, 4, 1, 5).reshape(2, 4, 4, 4, rest)


def local(
    image_rows, text_states, text_segment, item_segment, norm_gain, norm_shift, triple_weight, output_weight,
    query_weight, memory_weight, return_weight, up_weight, inner_bias, down_weight, outer_bias, cotangent,
):
    items, r, d = image_rows.shape
    t = items * r
    x = image_rows.reshape(t, d)
    cot = cotangent.reshape(t, d)
    core = lax.axis_index("c")
    c = core.reshape(1).astype(jnp.int32)
    tseg = text_segment.reshape(-1, 1)

    n = lax.iota(jnp.int32, d)
    low = n % 8
    yl, yh, px, pz, cs = (n // 8) % 2, (n // 16) % 2, (n // 32) % 4, (n // 128) % 4, n // 512
    source = ((((pz * 2 + yl) * 2 + (cs ^ core)) * 4 + px) * 2 + yh) * 8 + low
    perm = (lax.broadcasted_iota(jnp.int32, (d, d), 0) == source[None, :]).astype(BF)

    p, h1m, h1t = triple_forward(x, norm_gain[0:1], norm_shift[0:1], perm, triple_weight)
    p = lax.all_to_all(p, BLK, 0, 0).reshape(8, items, r, 384)
    o = attend(p)
    o = lax.all_to_all(o.reshape(8, t, 128), BLK, 0, 0)
    memory = jnp.dot(text_states, memory_weight, preferred_element_type=F32).astype(BF)
    y1, qc, y2, h3, om, ot, h2m, h2t, ocm, oct_, h3m, h3t = middle(
        item_segment, o, x, output_weight, norm_gain, norm_shift, query_weight, memory, tseg, return_weight, perm
    )
    gm, gt, du, inner, out, dy2, dgain2, dshift2, outer = mlp(
        c, h3, up_weight, inner_bias.reshape(1, -1), down_weight, outer_bias.reshape(1, -1), cot, y2, norm_gain
    )
    cot_p = to_partner(cot)
    down_part = down_grad_local(gm, to_partner(gt), cot, cot_p)
    up_part = rows_grad(h3m, to_partner(h3t), du, to_partner(du), "up_grad_local")
    down_sum = scatter_all(down_part.reshape(4, 4, 4, 32, d), "xzy")
    up_sum = scatter_all(up_part.reshape(4, 4, 4, 8, -1), "zxy")

    b2, dqc, b1, dy1, do, dm, dgain1, dshift1 = middle_back(
        item_segment, dy2, return_weight, qc, memory, tseg, query_weight, y1, norm_gain, output_weight
    )
    do = lax.all_to_all(do, BLK, 0, 0).reshape(8, items, r, 128)
    return_part = rows_grad(ocm, to_partner(oct_), b2, to_partner(b2), "return_grad_local")
    query_part = rows_grad(h2m, to_partner(h2t), dqc, to_partner(dqc), "query_grad_local")
    output_part = rows_grad(om, to_partner(ot), b1, to_partner(b1), "output_grad_local")

    dp = attend_back(p, do)
    dp = lax.all_to_all(dp.reshape(8, t, 384), BLK, 0, 0)
    input_grad, dgain0, dshift0, dp_flat = triple_back(dp, triple_weight, x, norm_gain, dy1)
    triple_part = triple_grad_local(h1m, to_partner(h1t), dp_flat, to_partner(dp_flat))
    triple_sum = scatter_all(triple_part.reshape(4, 4, 4, 8, 3 * d), "zxy")

    dm_rows = by_owner(dm.astype(BF), 2 * d).reshape(2, 4, 4, 4, 8, 2 * d // 8)
    rows = [dgain0, dgain1, dgain2, dshift0, dshift1, dshift2, outer, inner]
    thin = jnp.concatenate([by_owner(v.astype(BF), v.shape[1] // 128) for v in rows], axis=-1)
    used = thin.shape[-1]
    thin = jnp.pad(thin, ((0, 0),) * 4 + ((0, 1024 - used),)).reshape(2, 4, 4, 4, 8, 128)
    extra = jnp.concatenate([dm_rows, thin], axis=-1)
    theirs = lax.dynamic_index_in_dim(extra, 1 - core, 0, keepdims=False)
    extra = lax.dynamic_index_in_dim(extra, core, 0, keepdims=False).astype(F32) + to_partner(theirs).astype(F32)
    small = jnp.concatenate(
        [v.reshape(4, 4, 4, 8, d) for v in (return_part, query_part, output_part)] + [extra.astype(BF)], axis=-1
    )
    small_sum = scatter_all(small, "yzx")
    return_grad, query_grad, output_grad = (small_sum[:, i * d : (i + 1) * d] for i in range(3))
    dm_mine = small_sum[:, 3 * d : 3 * d + 2 * d // 8]
    thin_mine = small_sum[:, 3 * d + 2 * d // 8 :].reshape(-1)[:used]
    gains, shifts = thin_mine[:24].reshape(3, 8), thin_mine[24:48].reshape(3, 8)
    outer_mine, inner_mine = thin_mine[48:56], thin_mine[56:]
    dm_all = lax.all_to_all(jnp.broadcast_to(dm_mine.astype(BF), (128,) + dm_mine.shape), ALL, 0, 0)
    dm_all = dm_all.reshape(128, 2 * d)
    me = lax.axis_index(ALL)
    text_cols = lax.dynamic_slice_in_dim(text_states, me * 8, 8, 1)
    memory_rows = lax.dynamic_slice_in_dim(memory_weight, me * 8, 8, 0)
    memory_grad = dot(text_cols, dm_all, 0, 0)
    text_grad = dot(dm_all, memory_rows, 1, 1)
    return (
        out.reshape(items, r, d), input_grad.reshape(items, r, d), text_grad, gains, shifts, triple_sum, output_grad,
        query_grad, memory_grad, return_grad, up_sum, inner_mine, down_sum, outer_mine,
    )


def solution(mesh):
    fine = Mesh(mesh.devices.reshape(4, 2, 2, 4, 2), ALL)
    dp = ("z", "yl", "c")
    rows = P(dp, BLK, None)
    placed = (rows, P(), P(), P(dp)) + (P(),) * 11 + (rows,)
    outs = (
        rows, rows, P(None, ALL), P(None, ALL), P(None, ALL), P(ALL, None), P(ALL, None), P(ALL, None), P(ALL, None),
        P(ALL, None), P(ALL, None), P(ALL), P(ALL, None), P(ALL),
    )
    return jax.shard_map(local, mesh=fine, in_specs=placed, out_specs=outs, check_vma=False)
```

time: 1040 us -> 436 us (0.42)
  waiting for transfers between devices: 625 us -> 148 us
  matrix products: 146 us -> 5.59 us
  local copies, waits for them, and re-layouts: 156 us -> 57.1 us
  Pallas kernels: 0 us -> 89.8 us
  starting transfers between devices: 0.29 us -> 84.7 us
  other arithmetic: 56.4 us -> 13.6 us
  between operations: 17.3 us -> 1.95 us
    reduce_scatter x5 -> x0, waiting for transfers between devices: 522 us -> none  [the longest x3 430 us: side_by_side(): lax.psum_scatter(both, axis, scatter_dimension=dim, tiled=True)]
    dot_general x32 -> x3, matrix products: 142 us -> 5.59 us  [the longest x1 3.05 us: local(): jnp.dot(text_states, memory_weight, preferred_element_type=F32).astype(BF)]
    ppermute x0 -> x49, waiting for transfers between devices: none -> 132 us  [the longest x36 132 us: ring_scatter(): lax.ppermute(piece(k), RINGS[axis], ring_pairs(axis, k))]
    all_gather x1 -> x0, waiting for transfers between devices: 103 us -> none  [in_one_piece(): result, at, done = (lax.all_gather(both, axis, axis=dim, tiled=True), 0, [])]
    pallas_call x0 -> x13, Pallas kernels: none -> 89.8 us  [the longest x1 18.1 us: mlp(): pl.pallas_call(mlp_body, grid=(n,), in_specs=[SMEM, whole((t, d)), pl.Blo...]
    ppermute x0 -> x49, starting transfers between devices: none -> 63.8 us  [the longest x36 60.4 us: ring_scatter(): lax.ppermute(piece(k), RINGS[axis], ring_pairs(axis, k))]
    convert_element_type x21 -> x0, local copies, waits for them, and re-layouts: 37.7 us -> none  [the longest x1 6.62 us: local(): value_part.reshape(item_count, full_rows, model_width).astype(jnp.bfloat16)]
    unnamed x1 -> x0, blocking collectives: 30.4 us -> none
  transfers between devices with their start and end apart: 7 -> 53, of which waited for: 6 -> 21; matrix products, arithmetic and copies ran while one was open for 15% -> 8% of each run, Pallas kernels for 0% -> 10%
where the time goes in v1:
time: 436 us; the launch traced here: 430 us
  waiting for transfers between devices  148 us (34%)
  Pallas kernels  89.8 us (21%)
  starting transfers between devices  84.7 us (19%)
  local copies, waits for them, and re-layouts  57.1 us (13%)
  blocking collectives  29.3 us (7%)
  other arithmetic  13.6 us (3%)
  matrix products  5.59 us (1%)
    ppermute x36, waiting for transfers between devices, ring_scatter(): lax.ppermute(piece(k), RINGS[axis], ring_pairs(axis, k))  132 us
    ppermute x36, starting transfers between devices, ring_scatter(): lax.ppermute(piece(k), RINGS[axis], ring_pairs(axis, k))  60.4 us
    unnamed x124, local copies, waits for them, and re-layouts  38.4 us
    all_to_all x1, blocking collectives, local(): p = lax.all_to_all(p, BLK, 0, 0).reshape(8, items, r, 384)  29.3 us
    pallas_call x1, Pallas kernels, mlp(): pl.pallas_call(mlp_body, grid=(n,), in_specs=[SMEM, whole((t, d)), pl.Blo...  18.1 us
    pallas_call x4, Pallas kernels, rows_grad(): pl.pallas_call(rows_grad_body, grid=(n // tile,), in_specs=[whole((t, row...  13.4 us
    pallas_call x1, Pallas kernels, attend_back(): pl.pallas_call(attend_back_body, grid=(items,), in_specs=[pl.BlockSpec((b...  12.7 us
    pallas_call x1, Pallas kernels, attend(): pl.pallas_call(attend_body, grid=(items,), in_specs=[pl.BlockSpec((b, 1,...  10.1 us
  transfers between devices with their start and end apart: 53, of which 21 were waited for; matrix products, arithmetic and copies ran while one was open for 8% of the time, Pallas kernels for 10%

profile of v1, /device:TPU:0, one launch (start us, length us, event | category | flops | bytes accessed | tf_op | source)
XLA Modules:
  0.0 429.7 jit_solution(17749938558268435426)
XLA Ops:
  3.1 3.5 copy-done.1
  6.7 4.7 %triple_forward.1 = (bf16[8,256,384]{2,1,0:T(8,128)(2,1)S(1)}, bf16[256,512]{1,0:T(8,128)(2,1)S(1)}, bf16[256,512]{1,0:T(8,128)(2,1)}) custom-call(bf16[256,1024]{1,0:T(8,128)(2,1)S(1)} %bitcast.177, f32[1,1024]{1,0:T(1,128)S(1)} %slice.43.g_ref, f32[1,1024]{1,0:T(1,128)S(1)} %slice.44.s_ref, bf16[1024,1024]{1,0:T(8,128)(2,1)S(1)} %fusion.perm_ref, ...), custom_call_target="tpu_custom_call" | custom-call | flops 2147483648 | bytes 10485760 | tf_op jit(solution)/shard_map/triple_forward/pallas_call | solution.py:80
  11.4 29.3 %all_to_all.25 = bf16[8,256,384]{2,1,0:T(8,128)(2,1)S(1)} all-to-all(bf16[8,256,384]{2,1,0:T(8,128)(2,1)S(1)} %get-tuple-element.50), channel_id=1, replica_groups=mesh['z'=4,'yl'=2,'c'=2,'x'=4,'yh'=2] {'x','yh'}, dimensions={0} | all-to-all | bytes 3145728 | tf_op jit(solution)/shard_map/all_to_all | solution.py:667
  40.7 10.1 %attend.1 = bf16[8,2,128,128]{3,2,1,0:T(8,128)(2,1)} custom-call(bf16[8,2,128,384]{3,2,1,0:T(8,128)(2,1)S(1)} %bitcast.181), custom_call_target="tpu_custom_call" | custom-call | flops 1342177280 | bytes 3145728 | tf_op jit(solution)/shard_map/attend/pallas_call | solution.py:147
  50.8 4.7 %all-to-all-start.1 = ((bf16[8,256,128]{2,1,0:T(8,128)(2,1)}), bf16[8,256,128]{2,1,0:T(8,128)(2,1)}, u32[]{:S(2)}, u32[]{:S(2)}) async-start(bf16[8,256,128]{2,1,0:T(8,128)(2,1)} %bitcast.3), calls=%async_computation.1 | async-start | bytes 1048576 | tf_op jit(solution)/shard_map/all_to_all | solution.py:669
  55.6 3.0 convolution_convert_fusion.m_ref
  58.7 6.4 %all-to-all-done.1.o_ref = bf16[8,256,128]{2,1,0:T(8,128)(2,1)} async-done(((bf16[8,256,128]{2,1,0:T(8,128)(2,1)}), bf16[8,256,128]{2,1,0:T(8,128)(2,1)}, u32[]{:S(2)}, u32[]{:S(2)}) %all-to-all-start.1) | async-done | bytes 524320 | tf_op jit(solution)/shard_map/all_to_all | solution.py:669
  68.3 8.2 %middle.1 = (f32[256,1024]{1,0:T(8,128)S(1)}, bf16[256,1024]{1,0:T(8,128)(2,1)S(1)}, f32[256,1024]{1,0:T(8,128)S(1)}, bf16[256,1024]{1,0:T(8,128)(2,1)S(1)}, bf1...) custom-call(s32[2]{0:T(128)S(1)} %copy-done.48, ...), custom_call_target="tpu_custom_call" | custom-call | flops 3758096384 | bytes 14680064 | tf_op jit(solution)/shard_map/middle/pallas_call | solution.py:286
  76.7 18.1 %mlp.1 = (bf16[256,2048]{1,0:T(8,128)(2,1)S(1)}, bf16[256,2048]{1,0:T(8,128)(2,1)S(1)}, bf16[256,4096]{1,0:T(8,128)(2,1)}, f32[1,4096]{1,0:T(1,128)S(1)}, bf16[2...) custom-call(s32[1]{0:T(128)} %bitcast.c_ref, ...), custom_call_target="tpu_custom_call" | custom-call | flops 8589934592 | bytes 25165824 | tf_op jit(solution)/shard_map/mlp/pallas_call | solution.py:360
  94.9 6.6 %middle_back.1 = (bf16[256,1024]{1,0:T(8,128)(2,1)}, bf16[256,1024]{1,0:T(8,128)(2,1)}, bf16[256,1024]{1,0:T(8,128)(2,1)}, f32[256,1024]{1,0:T(8,128)S(1)}, bf16...) custom-call(s32[2]{0:T(128)S(1)} %copy-done.48, ...), custom_call_target="tpu_custom_call" | custom-call | flops 2147483648 | bytes 14680064 | tf_op jit(solution)/shard_map/middle_back/pallas_call | solution.py:452
  104.3 3.5 all-to-all-start.2
  108.4 9.0 %all-to-all-done.2 = bf16[8,256,128]{2,1,0:T(8,128)(2,1)S(1)} async-done(((bf16[8,256,128]{2,1,0:T(8,128)(2,1)}), bf16[8,256,128]{2,1,0:T(8,128)(2,1)S(1)}, u32[]{:S(2)}, u32[]{:S(2)}) %all-to-all-start.2) | async-done | bytes 524320 | tf_op jit(solution)/shard_map/all_to_all | solution.py:686
  118.8 12.7 %attend_back.1 = bf16[8,2,128,384]{3,2,1,0:T(8,128)(2,1)S(1)} custom-call(bf16[8,2,128,384]{3,2,1,0:T(8,128)(2,1)S(1)} %bitcast.182, bf16[8,2,128,128]{3,2,1,0:T(8,128)(2,1)S(1)} %bitcast.183), custom_call_target="tpu_custom_call" | custom-call | flops 3355443200 | bytes 5242880 | tf_op jit(solution)/shard_map/attend_back/pallas_call | solution.py:190
  132.7 3.7 all-to-all-start.3
  140.1 6.2 %down_grad_local.1 = bf16[4,4,2,2,32,1024]{5,4,3,2,1,0:T(8,128)(2,1)S(1)} custom-call(bf16[256,2048]{1,0:T(8,128)(2,1)S(1)} %copy-done.57, bf16[256,2048]{1,0:T(8,128)(2,1)} %collective-permute-done.38.gp_ref, bf16[256,1024]{1,0:T(8,128)(2,1)S(1)} %bitcast.186, bf16[256,1024]{1,0:T(8,128)(2,1)S(1)} %collective-permute-done.39.rp_ref), custom_call_target="tpu_custom_call" | custom-call | flops 2147483648 | bytes 10485760 | tf_op jit(solution)/shard_map/down_grad_local/pallas_call | solution.py:584
  151.0 3.2 collective-permute-start.42
  181.3 2.8 copy-done.2
  185.3 5.4 %triple_back.1 = (f32[256,1024]{1,0:T(8,128)}, f32[1,1024]{1,0:T(1,128)S(1)}, f32[1,1024]{1,0:T(1,128)S(1)}, bf16[3,256,1024]{2,1,0:T(8,128)(2,1)S(1)}) custom-call(bf16[8,256,384]{2,1,0:T(8,128)(2,1)S(1)} %all-to-all-done.3.dp_ref, bf16[1024,3072]{1,0:T(8,128)(2,1)S(1)} %copy-done.2, bf16[1024,3072]{1,0:T(8,128)(2,1)S(1)} %copy-done.2, ...), custom_call_target="tpu_custom_call" | custom-call | flops 1610612736 | bytes 12582912 | tf_op jit(solution)/shard_map/triple_back/pallas_call | solution.py:493
  195.8 5.2 %collective-permute-done.41 = bf16[4,4,32,1024]{3,2,1,0:T(8,128)(2,1)} collective-permute-done((bf16[4,4,32,1024]{3,2,1,0:T(8,128)(2,1)}, bf16[4,4,32,1024]{3,2,1,0:T(8,128)(2,1)}, u32[]{:S(2)}, u32[]{:S(2)}) %collective-permute-start.41) | collective-permute-done | bytes 1048608 | tf_op jit(solution)/shard_map/ppermute | solution.py:623
  201.0 3.1 fusion.3
  204.3 4.0 collective-permute-start.45
  211.0 4.4 %collective-permute-done.45 = bf16[4,32,1024]{2,1,0:T(8,128)(2,1)S(1)} collective-permute-done((bf16[4,32,1024]{2,1,0:T(8,128)(2,1)S(1)}, bf16[4,32,1024]{2,1,0:T(8,128)(2,1)S(1)}, u32[]{:S(2)}, u32[]{:S(2)}) %collective-permute-start.45) | collective-permute-done | bytes 262176 | tf_op jit(solution)/shard_map/ppermute | solution.py:623
  215.4 3.0 collective-permute-start.9
  218.4 2.5 collective-permute-done.44
  220.9 3.1 collective-permute-start.8
  226.5 6.9 %up_grad_local.1 = bf16[512,4096]{1,0:T(8,128)(2,1)S(1)} custom-call(bf16[256,512]{1,0:T(8,128)(2,1)S(1)} %copy-done.33, bf16[256,512]{1,0:T(8,128)(2,1)} %collective-permute-done.27.lp_ref, bf16[256,4096]{1,0:T(8,128)(2,1)} %get-tuple-element.83.rm_ref, bf16[256,4096]{1,0:T(8,128)(2,1)} %collective-permute-done.28.rp_ref), custom_call_target="tpu_custom_call" | custom-call | flops 2147483648 | bytes 8388608 | tf_op jit(solution)/shard_map/up_grad_local/pallas_call | solution.py:535
  234.5 22.7 %collective-permute-done.48 = bf16[32,1024]{1,0:T(8,128)(2,1)S(1)} collective-permute-done((bf16[32,1024]{1,0:T(8,128)(2,1)S(1)}, bf16[32,1024]{1,0:T(8,128)(2,1)S(1)}, u32[]{:S(2)}, u32[]{:S(2)}) %collective-permute-start.48) | collective-permute-done | bytes 65568 | tf_op jit(solution)/shard_map/ppermute | solution.py:623
  259.2 4.2 collective-permute-done.46
  264.1 2.9 collective-permute-start.31
  269.6 22.0 %collective-permute-done.31 = bf16[4,4,8,4096]{3,2,1,0:T(8,128)(2,1)S(1)} collective-permute-done((bf16[4,4,8,4096]{3,2,1,0:T(8,128)(2,1)S(1)}, bf16[4,4,8,4096]{3,2,1,0:T(8,128)(2,1)S(1)}, u32[]{:S(2)}, u32[]{:S(2)}) %collective-permute-start.31) | collective-permute-done | bytes 1048608 | tf_op jit(solution)/shard_map/ppermute | solution.py:623
  291.6 2.9 collective-permute-start.12
  294.5 20.0 %collective-permute-done.30 = bf16[4,4,8,4096]{3,2,1,0:T(8,128)(2,1)S(1)} collective-permute-done((bf16[4,4,8,4096]{3,2,1,0:T(8,128)(2,1)S(1)}, bf16[4,4,8,4096]{3,2,1,0:T(8,128)(2,1)S(1)}, u32[]{:S(2)}, u32[]{:S(2)}) %collective-permute-start.30) | collective-permute-done | bytes 1048608 | tf_op jit(solution)/shard_map/ppermute | solution.py:623
  314.5 2.5 collective-permute-start.11
  318.4 5.2 %collective-permute-done.11 = bf16[4,8,3456]{2,1,0:T(8,128)(2,1)S(1)} collective-permute-done((bf16[4,8,3456]{2,1,0:T(8,128)(2,1)S(1)}, bf16[4,8,3456]{2,1,0:T(8,128)(2,1)S(1)}, u32[]{:S(2)}, u32[]{:S(2)}) %collective-permute-start.11) | collective-permute-done | bytes 221216 | tf_op jit(solution)/shard_map/ppermute | solution.py:623
  325.2 3.3 collective-permute-start.15
  331.4 2.7 collective-permute-start.34
  335.2 3.0 collective-permute-done.13
  339.7 9.1 %all-to-all-start.4 = ((bf16[128,8,256]{2,1,0:T(8,128)(2,1)}), bf16[128,8,256]{2,1,0:T(8,128)(2,1)}, u32[]{:S(2)}, u32[]{:S(2)}) async-start(bf16[128,8,256]{2,1,0:T(8,128)(2,1)} %broadcast_in_dim.4), calls=%async_computation.4 | async-start | bytes 1048576 | tf_op jit(solution)/shard_map/all_to_all | solution.py:714
  355.5 4.3 %triple_grad_local.1 = bf16[512,3072]{1,0:T(8,128)(2,1)S(1)} custom-call(bf16[256,512]{1,0:T(8,128)(2,1)S(1)} %copy-done.45, bf16[256,512]{1,0:T(8,128)(2,1)} %collective-permute-done.16.lp_ref, bf16[3,256,1024]{2,1,0:T(8,128)(2,1)S(1)} %copy-done.20, bf16[3,256,1024]{2,1,0:T(8,128)(2,1)S(1)} %copy-done.22), custom_call_target="tpu_custom_call" | custom-call | flops 1610612736 | bytes 6291456 | tf_op jit(solution)/shard_map/triple_grad_local/pallas_call | solution.py:558
  361.2 2.5 collective-permute-start.37
  367.2 3.5 collective-permute-start.20
  374.8 14.8 %collective-permute-done.20 = bf16[4,4,8,3072]{3,2,1,0:T(8,128)(2,1)} collective-permute-done((bf16[4,4,8,3072]{3,2,1,0:T(8,128)(2,1)}, bf16[4,4,8,3072]{3,2,1,0:T(8,128)(2,1)}, u32[]{:S(2)}, u32[]{:S(2)}) %collective-permute-start.20) | collective-permute-done | bytes 786464 | tf_op jit(solution)/shard_map/ppermute | solution.py:623
  389.5 15.9 %collective-permute-done.19 = bf16[4,4,8,3072]{3,2,1,0:T(8,128)(2,1)} collective-permute-done((bf16[4,4,8,3072]{3,2,1,0:T(8,128)(2,1)}, bf16[4,4,8,3072]{3,2,1,0:T(8,128)(2,1)}, u32[]{:S(2)}, u32[]{:S(2)}) %collective-permute-start.19) | collective-permute-done | bytes 786464 | tf_op jit(solution)/shard_map/ppermute | solution.py:623
  407.6 3.1 collective-permute-start.23
  413.7 3.4 collective-permute-done.23
  417.0 2.7 collective-permute-done.22
  421.2 2.3 collective-permute-start.25
  426.0 2.8 collective-permute-done.24
  (268 shorter events, 98.5 us)
Async XLA Ops:
  50.8 14.4 %all-to-all-start.1 = ((bf16[8,256,128]{2,1,0:T(8,128)(2,1)}), bf16[8,256,128]{2,1,0:T(8,128)(2,1)}, u32[]{:S(2)}, u32[]{:S(2)}) async-start(bf16[8,256,128]{2,1,0:T(8,128)(2,1)} %bitcast.3), calls=%async_computation.1 | async-start | bytes 1048576 | tf_op jit(solution)/shard_map/all_to_all | solution.py:669
  104.3 13.1 %all-to-all-start.2 = ((bf16[8,256,128]{2,1,0:T(8,128)(2,1)}), bf16[8,256,128]{2,1,0:T(8,128)(2,1)S(1)}, u32[]{:S(2)}, u32[]{:S(2)}) async-start(bf16[8,256,128]{2,1,0:T(8,128)(2,1)} %copy-done.31), calls=%async_computation.2 | async-start | bytes 1048576 | tf_op jit(solution)/shard_map/all_to_all | solution.py:686
  107.8 31.0 %collective-permute-start.38 = (bf16[256,2048]{1,0:T(8,128)(2,1)}, bf16[256,2048]{1,0:T(8,128)(2,1)}, u32[]{:S(2)}, u32[]{:S(2)}) collective-permute-start(bf16[256,2048]{1,0:T(8,128)(2,1)} %copy-done.49), channel_id=1, source_target_pairs={{0,8},{8,0},{1,9},{9,1},{2,10},{10,2},{3,11},{11,3},{4,12},{12,4},... | collective-permute-start | bytes 3145736 | tf_op jit(solution)/shard_map/ppermute | solution.py:640
  107.9 30.4 %collective-permute-start.39 = (bf16[256,1024]{1,0:T(8,128)(2,1)}, bf16[256,1024]{1,0:T(8,128)(2,1)S(1)}, u32[]{:S(2)}, u32[]{:S(2)}) collective-permute-start(bf16[256,1024]{1,0:T(8,128)(2,1)} %bitcast.184), channel_id=1, source_target_pairs={{0,8},{8,0},{1,9},{9,1},{2,10},{10,2},{3,11},{11,3},{4,12},{12,4},... | collective-permute-start | bytes 1572872 | tf_op jit(solution)/shard_map/ppermute | solution.py:640
  132.7 48.6 %all-to-all-start.3 = ((bf16[8,256,384]{2,1,0:T(8,128)(2,1)}), bf16[8,256,384]{2,1,0:T(8,128)(2,1)S(1)}, u32[]{:S(2)}, u32[]{:S(2)}) async-start(bf16[8,256,384]{2,1,0:T(8,128)(2,1)} %bitcast.180), calls=%async_computation.3 | async-start | bytes 3145728 | tf_op jit(solution)/shard_map/all_to_all | solution.py:692
  136.6 19.5 %collective-permute-start.1 = (bf16[256,1024]{1,0:T(8,128)(2,1)}, bf16[256,1024]{1,0:T(8,128)(2,1)S(1)}, u32[]{:S(2)}, u32[]{:S(2)}) collective-permute-start(bf16[256,1024]{1,0:T(8,128)(2,1)} %get-tuple-element.62.rm_ref), channel_id=1, source_target_pairs={{0,8},{8,0},{1,9},{9,1},{2,10},{10,2},{3,11},{11,3},{4,12},{12,4},... | collective-permute-start | bytes 1572872 | tf_op jit(solution)/shard_map/ppermute | solution.py:640
  137.3 13.0 %collective-permute-start = (bf16[256,512]{1,0:T(8,128)(2,1)}, bf16[256,512]{1,0:T(8,128)(2,1)S(1)}, u32[]{:S(2)}, u32[]{:S(2)}) collective-permute-start(bf16[256,512]{1,0:T(8,128)(2,1)} %copy-done.53), channel_id=1, source_target_pairs={{0,8},{8,0},{1,9},{9,1},{2,10},{10,2},{3,11},{11,3},{4,12},{12,4},... | collective-permute-start | bytes 786440 | tf_op jit(solution)/shard_map/ppermute | solution.py:640
  138.2 20.1 %collective-permute-start.3 = (bf16[256,1024]{1,0:T(8,128)(2,1)}, bf16[256,1024]{1,0:T(8,128)(2,1)S(1)}, u32[]{:S(2)}, u32[]{:S(2)}) collective-permute-start(bf16[256,1024]{1,0:T(8,128)(2,1)} %get-tuple-element.65.rm_ref), channel_id=1, source_target_pairs={{0,8},{8,0},{1,9},{9,1},{2,10},{10,2},{3,11},{11,3},{4,12},{12,4},... | collective-permute-start | bytes 1572872 | tf_op jit(solution)/shard_map/ppermute | solution.py:640
  138.3 15.8 %collective-permute-start.2 = (bf16[256,512]{1,0:T(8,128)(2,1)}, bf16[256,512]{1,0:T(8,128)(2,1)S(1)}, u32[]{:S(2)}, u32[]{:S(2)}) collective-permute-start(bf16[256,512]{1,0:T(8,128)(2,1)} %copy-done.52), channel_id=1, source_target_pairs={{0,8},{8,0},{1,9},{9,1},{2,10},{10,2},{3,11},{11,3},{4,12},{12,4},... | collective-permute-start | bytes 786440 | tf_op jit(solution)/shard_map/ppermute | solution.py:640
  138.8 39.1 %collective-permute-start.5 = (bf16[256,1024]{1,0:T(8,128)(2,1)}, bf16[256,1024]{1,0:T(8,128)(2,1)}, u32[]{:S(2)}, u32[]{:S(2)}) collective-permute-start(bf16[256,1024]{1,0:T(8,128)(2,1)} %get-tuple-element.68.rm_ref), channel_id=1, source_target_pairs={{0,8},{8,0},{1,9},{9,1},{2,10},{10,2},{3,11},{11,3},{4,12},{12,4},... | collective-permute-start | bytes 1572872 | tf_op jit(solution)/shard_map/ppermute | solution.py:640
  151.0 44.3 %collective-permute-start.42 = (bf16[4,4,32,1024]{3,2,1,0:T(8,128)(2,1)}, bf16[4,4,32,1024]{3,2,1,0:T(8,128)(2,1)}, u32[]{:S(2)}, u32[]{:S(2)}) collective-permute-start(bf16[4,4,32,1024]{3,2,1,0:T(8,128)(2,1)} %get-tuple-element.87), channel_id=1, source_target_pairs={{0,4},{2,6},{4,0},{6,2},{1,5},{3,7},{5,1},{7,3},{8,12},{10,14},{12... | collective-permute-start | bytes 3145736 | tf_op jit(solution)/shard_map/ppermute | solution.py:623
  154.9 46.2 %collective-permute-start.41 = (bf16[4,4,32,1024]{3,2,1,0:T(8,128)(2,1)}, bf16[4,4,32,1024]{3,2,1,0:T(8,128)(2,1)}, u32[]{:S(2)}, u32[]{:S(2)}) collective-permute-start(bf16[4,4,32,1024]{3,2,1,0:T(8,128)(2,1)} %get-tuple-element.88), channel_id=1, source_target_pairs={{0,6},{2,0},{4,2},{6,4},{1,7},{3,1},{5,3},{7,5},{8,14},{10,8},{12,... | collective-permute-start | bytes 3145736 | tf_op jit(solution)/shard_map/ppermute | solution.py:623
  156.9 44.2 %collective-permute-start.40 = (bf16[4,4,32,1024]{3,2,1,0:T(8,128)(2,1)}, bf16[4,4,32,1024]{3,2,1,0:T(8,128)(2,1)}, u32[]{:S(2)}, u32[]{:S(2)}) collective-permute-start(bf16[4,4,32,1024]{3,2,1,0:T(8,128)(2,1)} %get-tuple-element.86), channel_id=1, source_target_pairs={{0,2},{2,4},{4,6},{6,0},{1,3},{3,5},{5,7},{7,1},{8,10},{10,12},{12... | collective-permute-start | bytes 3145736 | tf_op jit(solution)/shard_map/ppermute | solution.py:623
  159.1 18.3 %collective-permute-start.4 = (bf16[256,512]{1,0:T(8,128)(2,1)}, bf16[256,512]{1,0:T(8,128)(2,1)}, u32[]{:S(2)}, u32[]{:S(2)}) collective-permute-start(bf16[256,512]{1,0:T(8,128)(2,1)} %get-tuple-element.67), channel_id=1, source_target_pairs={{0,8},{8,0},{1,9},{9,1},{2,10},{10,2},{3,11},{11,3},{4,12},{12,4},... | collective-permute-start | bytes 786440 | tf_op jit(solution)/shard_map/ppermute | solution.py:640
  177.4 46.8 %collective-permute-start.27 = (bf16[256,512]{1,0:T(8,128)(2,1)}, bf16[256,512]{1,0:T(8,128)(2,1)}, u32[]{:S(2)}, u32[]{:S(2)}) collective-permute-start(bf16[256,512]{1,0:T(8,128)(2,1)} %get-tuple-element.82), channel_id=1, source_target_pairs={{0,8},{8,0},{1,9},{9,1},{2,10},{10,2},{3,11},{11,3},{4,12},{12,4},... | collective-permute-start | bytes 786440 | tf_op jit(solution)/shard_map/ppermute | solution.py:640
  177.9 48.6 %collective-permute-start.28 = (bf16[256,4096]{1,0:T(8,128)(2,1)}, bf16[256,4096]{1,0:T(8,128)(2,1)}, u32[]{:S(2)}, u32[]{:S(2)}) collective-permute-start(bf16[256,4096]{1,0:T(8,128)(2,1)} %get-tuple-element.83.rm_ref), channel_id=1, source_target_pairs={{0,8},{8,0},{1,9},{9,1},{2,10},{10,2},{3,11},{11,3},{4,12},{12,4},... | collective-permute-start | bytes 6291464 | tf_op jit(solution)/shard_map/ppermute | solution.py:640
  195.3 13.7 %collective-permute-start.6 = (bf16[4,4,4,8,384]{4,3,1,0,2:T(8,128)(2,1)S(1)}, bf16[4,4,4,8,384]{4,3,1,0,2:T(8,128)(2,1)S(1)}, u32[]{:S(2)}, u32[]{:S(2)}) collective-permute-start(bf16[4,4,4,8,384]{4,3,1,0,2:T(8,128)(2,1)S(1)} %dynamic-slice_bitcast_fusion.12), channel_id=1, source_target_pairs={{0,8},{8,0},{1,9},{9,1},{2,10},{10,2},{3,11},{11,3},{4,12},{12,4},... | collective-permute-start | bytes 1179656 | tf_op jit(solution)/shard_map/ppermute | solution.py:640
  204.3 11.1 %collective-permute-start.45 = (bf16[4,32,1024]{2,1,0:T(8,128)(2,1)S(1)}, bf16[4,32,1024]{2,1,0:T(8,128)(2,1)S(1)}, u32[]{:S(2)}, u32[]{:S(2)}) collective-permute-start(bf16[4,32,1024]{2,1,0:T(8,128)(2,1)S(1)} %get-tuple-element.99), channel_id=1, source_target_pairs={{0,64},{32,96},{64,0},{96,32},{1,65},{33,97},{65,1},{97,33},{2,66}... | collective-permute-start | bytes 786440 | tf_op jit(solution)/shard_map/ppermute | solution.py:623
  208.2 12.6 %collective-permute-start.44 = (bf16[4,32,1024]{2,1,0:T(8,128)(2,1)S(1)}, bf16[4,32,1024]{2,1,0:T(8,128)(2,1)S(1)}, u32[]{:S(2)}, u32[]{:S(2)}) collective-permute-start(bf16[4,32,1024]{2,1,0:T(8,128)(2,1)S(1)} %get-tuple-element.100), channel_id=1, source_target_pairs={{0,96},{32,0},{64,32},{96,64},{1,97},{33,1},{65,33},{97,65},{2,98}... | collective-permute-start | bytes 786440 | tf_op jit(solution)/shard_map/ppermute | solution.py:623
  209.0 15.0 %collective-permute-start.43 = (bf16[4,32,1024]{2,1,0:T(8,128)(2,1)S(1)}, bf16[4,32,1024]{2,1,0:T(8,128)(2,1)S(1)}, u32[]{:S(2)}, u32[]{:S(2)}) collective-permute-start(bf16[4,32,1024]{2,1,0:T(8,128)(2,1)S(1)} %get-tuple-element.98), channel_id=1, source_target_pairs={{0,32},{32,64},{64,96},{96,0},{1,33},{33,65},{65,97},{97,1},{2,34}... | collective-permute-start | bytes 786440 | tf_op jit(solution)/shard_map/ppermute | solution.py:623
  215.4 48.7 %collective-permute-start.9 = (bf16[4,4,8,3456]{3,2,1,0:T(8,128)(2,1)S(1)}, bf16[4,4,8,3456]{3,2,1,0:T(8,128)(2,1)S(1)}, u32[]{:S(2)}, u32[]{:S(2)}) collective-permute-start(bf16[4,4,8,3456]{3,2,1,0:T(8,128)(2,1)S(1)} %get-tuple-element.93), channel_id=1, source_target_pairs={{0,1},{16,17},{1,0},{17,16},{2,3},{18,19},{3,2},{19,18},{4,5},{20,... | collective-permute-start | bytes 2654216 | tf_op jit(solution)/shard_map/ppermute | solution.py:623
  220.9 46.1 %collective-permute-start.8 = (bf16[4,4,8,3456]{3,2,1,0:T(8,128)(2,1)S(1)}, bf16[4,4,8,3456]{3,2,1,0:T(8,128)(2,1)S(1)}, u32[]{:S(2)}, u32[]{:S(2)}) collective-permute-start(bf16[4,4,8,3456]{3,2,1,0:T(8,128)(2,1)S(1)} %get-tuple-element.94), channel_id=1, source_target_pairs={{0,17},{16,0},{1,16},{17,1},{2,19},{18,2},{3,18},{19,3},{4,21},{20... | collective-permute-start | bytes 2654216 | tf_op jit(solution)/shard_map/ppermute | solution.py:623
  224.0 43.7 %collective-permute-start.7 = (bf16[4,4,8,3456]{3,2,1,0:T(8,128)(2,1)S(1)}, bf16[4,4,8,3456]{3,2,1,0:T(8,128)(2,1)S(1)}, u32[]{:S(2)}, u32[]{:S(2)}) collective-permute-start(bf16[4,4,8,3456]{3,2,1,0:T(8,128)(2,1)S(1)} %get-tuple-element.92), channel_id=1, source_target_pairs={{0,16},{16,1},{1,17},{17,0},{2,18},{18,3},{3,19},{19,2},{4,20},{20... | collective-permute-start | bytes 2654216 | tf_op jit(solution)/shard_map/ppermute | solution.py:623
  224.2 33.0 %collective-permute-start.48 = (bf16[32,1024]{1,0:T(8,128)(2,1)S(1)}, bf16[32,1024]{1,0:T(8,128)(2,1)S(1)}, u32[]{:S(2)}, u32[]{:S(2)}) collective-permute-start(bf16[32,1024]{1,0:T(8,128)(2,1)S(1)} %get-tuple-element.111), channel_id=1, source_target_pairs={{0,1},{16,17},{1,0},{17,16},{2,3},{18,19},{3,2},{19,18},{4,5},{20,... | collective-permute-start | bytes 196616 | tf_op jit(solution)/shard_map/ppermute | solution.py:623
  233.4 25.7 %collective-permute-start.47 = (bf16[32,1024]{1,0:T(8,128)(2,1)S(1)}, bf16[32,1024]{1,0:T(8,128)(2,1)S(1)}, u32[]{:S(2)}, u32[]{:S(2)}) collective-permute-start(bf16[32,1024]{1,0:T(8,128)(2,1)S(1)} %get-tuple-element.112), channel_id=1, source_target_pairs={{0,17},{16,0},{1,16},{17,1},{2,19},{18,2},{3,18},{19,3},{4,21},{20... | collective-permute-start | bytes 196616 | tf_op jit(solution)/shard_map/ppermute | solution.py:623
  259.1 91.5 %collective-permute-start.16 = (bf16[256,512]{1,0:T(8,128)(2,1)}, bf16[256,512]{1,0:T(8,128)(2,1)}, u32[]{:S(2)}, u32[]{:S(2)}) collective-permute-start(bf16[256,512]{1,0:T(8,128)(2,1)} %get-tuple-element.79), channel_id=1, source_target_pairs={{0,8},{8,0},{1,9},{9,1},{2,10},{10,2},{3,11},{11,3},{4,12},{12,4},... | collective-permute-start | bytes 786440 | tf_op jit(solution)/shard_map/ppermute | solution.py:640
  263.4 87.3 %collective-permute-start.17 = (bf16[3,256,1024]{2,1,0:T(8,128)(2,1)S(1)}, bf16[3,256,1024]{2,1,0:T(8,128)(2,1)S(1)}, u32[]{:S(2)}, u32[]{:S(2)}) collective-permute-start(bf16[3,256,1024]{2,1,0:T(8,128)(2,1)S(1)} %copy-done.19), channel_id=1, source_target_pairs={{0,8},{8,0},{1,9},{9,1},{2,10},{10,2},{3,11},{11,3},{4,12},{12,4},... | collective-permute-start | bytes 4718600 | tf_op jit(solution)/shard_map/ppermute | solution.py:640
  264.1 27.5 %collective-permute-start.31 = (bf16[4,4,8,4096]{3,2,1,0:T(8,128)(2,1)S(1)}, bf16[4,4,8,4096]{3,2,1,0:T(8,128)(2,1)S(1)}, u32[]{:S(2)}, u32[]{:S(2)}) collective-permute-start(bf16[4,4,8,4096]{3,2,1,0:T(8,128)(2,1)S(1)} %get-tuple-element.90), channel_id=1, source_target_pairs={{0,64},{32,96},{64,0},{96,32},{1,65},{33,97},{65,1},{97,33},{2,66}... | collective-permute-start | bytes 3145736 | tf_op jit(solution)/shard_map/ppermute | solution.py:623
  267.0 47.5 %collective-permute-start.30 = (bf16[4,4,8,4096]{3,2,1,0:T(8,128)(2,1)S(1)}, bf16[4,4,8,4096]{3,2,1,0:T(8,128)(2,1)S(1)}, u32[]{:S(2)}, u32[]{:S(2)}) collective-permute-start(bf16[4,4,8,4096]{3,2,1,0:T(8,128)(2,1)S(1)} %get-tuple-element.91), channel_id=1, source_target_pairs={{0,96},{32,0},{64,32},{96,64},{1,97},{33,1},{65,33},{97,65},{2,98}... | collective-permute-start | bytes 3145736 | tf_op jit(solution)/shard_map/ppermute | solution.py:623
  267.7 49.2 %collective-permute-start.29 = (bf16[4,4,8,4096]{3,2,1,0:T(8,128)(2,1)S(1)}, bf16[4,4,8,4096]{3,2,1,0:T(8,128)(2,1)S(1)}, u32[]{:S(2)}, u32[]{:S(2)}) collective-permute-start(bf16[4,4,8,4096]{3,2,1,0:T(8,128)(2,1)S(1)} %get-tuple-element.89), channel_id=1, source_target_pairs={{0,32},{32,64},{64,96},{96,0},{1,33},{33,65},{65,97},{97,1},{2,34}... | collective-permute-start | bytes 3145736 | tf_op jit(solution)/shard_map/ppermute | solution.py:623
  291.6 26.8 %collective-permute-start.12 = (bf16[4,8,3456]{2,1,0:T(8,128)(2,1)S(1)}, bf16[4,8,3456]{2,1,0:T(8,128)(2,1)S(1)}, u32[]{:S(2)}, u32[]{:S(2)}) collective-permute-start(bf16[4,8,3456]{2,1,0:T(8,128)(2,1)S(1)} %get-tuple-element.105), channel_id=1, source_target_pairs={{0,64},{32,96},{64,0},{96,32},{1,65},{33,97},{65,1},{97,33},{2,66}... | collective-permute-start | bytes 663560 | tf_op jit(solution)/shard_map/ppermute | solution.py:623
  314.5 9.1 %collective-permute-start.11 = (bf16[4,8,3456]{2,1,0:T(8,128)(2,1)S(1)}, bf16[4,8,3456]{2,1,0:T(8,128)(2,1)S(1)}, u32[]{:S(2)}, u32[]{:S(2)}) collective-permute-start(bf16[4,8,3456]{2,1,0:T(8,128)(2,1)S(1)} %get-tuple-element.106), channel_id=1, source_target_pairs={{0,96},{32,0},{64,32},{96,64},{1,97},{33,1},{65,33},{97,65},{2,98}... | collective-permute-start | bytes 663560 | tf_op jit(solution)/shard_map/ppermute | solution.py:623
  317.0 8.1 %collective-permute-start.10 = (bf16[4,8,3456]{2,1,0:T(8,128)(2,1)S(1)}, bf16[4,8,3456]{2,1,0:T(8,128)(2,1)S(1)}, u32[]{:S(2)}, u32[]{:S(2)}) collective-permute-start(bf16[4,8,3456]{2,1,0:T(8,128)(2,1)S(1)} %get-tuple-element.104), channel_id=1, source_target_pairs={{0,32},{32,64},{64,96},{96,0},{1,33},{33,65},{65,97},{97,1},{2,34}... | collective-permute-start | bytes 663560 | tf_op jit(solution)/shard_map/ppermute | solution.py:623
  325.2 6.3 %collective-permute-start.15 = (bf16[8,3456]{1,0:T(8,128)(2,1)S(1)}, bf16[8,3456]{1,0:T(8,128)(2,1)S(1)}, u32[]{:S(2)}, u32[]{:S(2)}) collective-permute-start(bf16[8,3456]{1,0:T(8,128)(2,1)S(1)} %get-tuple-element.117), channel_id=1, source_target_pairs={{0,4},{2,6},{4,0},{6,2},{1,5},{3,7},{5,1},{7,3},{8,12},{10,14},{12... | collective-permute-start | bytes 165896 | tf_op jit(solution)/shard_map/ppermute | solution.py:623
  329.6 8.6 %collective-permute-start.13 = (bf16[8,3456]{1,0:T(8,128)(2,1)S(1)}, bf16[8,3456]{1,0:T(8,128)(2,1)S(1)}, u32[]{:S(2)}, u32[]{:S(2)}) collective-permute-start(bf16[8,3456]{1,0:T(8,128)(2,1)S(1)} %get-tuple-element.116), channel_id=1, source_target_pairs={{0,2},{2,4},{4,6},{6,0},{1,3},{3,5},{5,7},{7,1},{8,10},{10,12},{12... | collective-permute-start | bytes 165896 | tf_op jit(solution)/shard_map/ppermute | solution.py:623
  331.4 28.4 %collective-permute-start.34 = (bf16[4,8,4096]{2,1,0:T(8,128)(2,1)}, bf16[4,8,4096]{2,1,0:T(8,128)(2,1)}, u32[]{:S(2)}, u32[]{:S(2)}) collective-permute-start(bf16[4,8,4096]{2,1,0:T(8,128)(2,1)} %get-tuple-element.102), channel_id=1, source_target_pairs={{0,4},{2,6},{4,0},{6,2},{1,5},{3,7},{5,1},{7,3},{8,12},{10,14},{12... | collective-permute-start | bytes 786440 | tf_op jit(solution)/shard_map/ppermute | solution.py:623
  334.2 25.7 %collective-permute-start.33 = (bf16[4,8,4096]{2,1,0:T(8,128)(2,1)}, bf16[4,8,4096]{2,1,0:T(8,128)(2,1)}, u32[]{:S(2)}, u32[]{:S(2)}) collective-permute-start(bf16[4,8,4096]{2,1,0:T(8,128)(2,1)} %get-tuple-element.103), channel_id=1, source_target_pairs={{0,6},{2,0},{4,2},{6,4},{1,7},{3,1},{5,3},{7,5},{8,14},{10,8},{12,... | collective-permute-start | bytes 786440 | tf_op jit(solution)/shard_map/ppermute | solution.py:623
  338.2 21.7 %collective-permute-start.32 = (bf16[4,8,4096]{2,1,0:T(8,128)(2,1)}, bf16[4,8,4096]{2,1,0:T(8,128)(2,1)}, u32[]{:S(2)}, u32[]{:S(2)}) collective-permute-start(bf16[4,8,4096]{2,1,0:T(8,128)(2,1)} %get-tuple-element.101), channel_id=1, source_target_pairs={{0,2},{2,4},{4,6},{6,0},{1,3},{3,5},{5,7},{7,1},{8,10},{10,12},{12... | collective-permute-start | bytes 786440 | tf_op jit(solution)/shard_map/ppermute | solution.py:623
  339.7 33.9 %all-to-all-start.4 = ((bf16[128,8,256]{2,1,0:T(8,128)(2,1)}), bf16[128,8,256]{2,1,0:T(8,128)(2,1)}, u32[]{:S(2)}, u32[]{:S(2)}) async-start(bf16[128,8,256]{2,1,0:T(8,128)(2,1)} %broadcast_in_dim.4), calls=%async_computation.4 | async-start | bytes 1048576 | tf_op jit(solution)/shard_map/all_to_all | solution.py:714
  361.2 10.5 %collective-permute-start.37 = (bf16[8,4096]{1,0:T(8,128)(2,1)S(1)}, bf16[8,4096]{1,0:T(8,128)(2,1)S(1)}, u32[]{:S(2)}, u32[]{:S(2)}) collective-permute-start(bf16[8,4096]{1,0:T(8,128)(2,1)S(1)} %get-tuple-element.114), channel_id=1, source_target_pairs={{0,1},{16,17},{1,0},{17,16},{2,3},{18,19},{3,2},{19,18},{4,5},{20,... | collective-permute-start | bytes 196616 | tf_op jit(solution)/shard_map/ppermute | solution.py:623
  363.7 9.2 %collective-permute-start.36 = (bf16[8,4096]{1,0:T(8,128)(2,1)S(1)}, bf16[8,4096]{1,0:T(8,128)(2,1)S(1)}, u32[]{:S(2)}, u32[]{:S(2)}) collective-permute-start(bf16[8,4096]{1,0:T(8,128)(2,1)S(1)} %get-tuple-element.115), channel_id=1, source_target_pairs={{0,17},{16,0},{1,16},{17,1},{2,19},{18,2},{3,18},{19,3},{4,21},{20... | collective-permute-start | bytes 196616 | tf_op jit(solution)/shard_map/ppermute | solution.py:623
  364.9 8.0 %collective-permute-start.35 = (bf16[8,4096]{1,0:T(8,128)(2,1)S(1)}, bf16[8,4096]{1,0:T(8,128)(2,1)S(1)}, u32[]{:S(2)}, u32[]{:S(2)}) collective-permute-start(bf16[8,4096]{1,0:T(8,128)(2,1)S(1)} %get-tuple-element.113), channel_id=1, source_target_pairs={{0,16},{16,1},{1,17},{17,0},{2,18},{18,3},{3,19},{19,2},{4,20},{20... | collective-permute-start | bytes 196616 | tf_op jit(solution)/shard_map/ppermute | solution.py:623
  367.2 22.3 %collective-permute-start.20 = (bf16[4,4,8,3072]{3,2,1,0:T(8,128)(2,1)}, bf16[4,4,8,3072]{3,2,1,0:T(8,128)(2,1)}, u32[]{:S(2)}, u32[]{:S(2)}) collective-permute-start(bf16[4,4,8,3072]{3,2,1,0:T(8,128)(2,1)} %get-tuple-element.96), channel_id=1, source_target_pairs={{0,64},{32,96},{64,0},{96,32},{1,65},{33,97},{65,1},{97,33},{2,66}... | collective-permute-start | bytes 2359304 | tf_op jit(solution)/shard_map/ppermute | solution.py:623
  370.7 34.8 %collective-permute-start.19 = (bf16[4,4,8,3072]{3,2,1,0:T(8,128)(2,1)}, bf16[4,4,8,3072]{3,2,1,0:T(8,128)(2,1)}, u32[]{:S(2)}, u32[]{:S(2)}) collective-permute-start(bf16[4,4,8,3072]{3,2,1,0:T(8,128)(2,1)} %get-tuple-element.97), channel_id=1, source_target_pairs={{0,96},{32,0},{64,32},{96,64},{1,97},{33,1},{65,33},{97,65},{2,98}... | collective-permute-start | bytes 2359304 | tf_op jit(solution)/shard_map/ppermute | solution.py:623
  371.8 33.7 %collective-permute-start.18 = (bf16[4,4,8,3072]{3,2,1,0:T(8,128)(2,1)}, bf16[4,4,8,3072]{3,2,1,0:T(8,128)(2,1)}, u32[]{:S(2)}, u32[]{:S(2)}) collective-permute-start(bf16[4,4,8,3072]{3,2,1,0:T(8,128)(2,1)} %get-tuple-element.95), channel_id=1, source_target_pairs={{0,32},{32,64},{64,96},{96,0},{1,33},{33,65},{65,97},{97,1},{2,34}... | collective-permute-start | bytes 2359304 | tf_op jit(solution)/shard_map/ppermute | solution.py:623
  407.6 9.4 %collective-permute-start.23 = (bf16[4,8,3072]{2,1,0:T(8,128)(2,1)S(1)}, bf16[4,8,3072]{2,1,0:T(8,128)(2,1)S(1)}, u32[]{:S(2)}, u32[]{:S(2)}) collective-permute-start(bf16[4,8,3072]{2,1,0:T(8,128)(2,1)S(1)} %get-tuple-element.108), channel_id=1, source_target_pairs={{0,4},{2,6},{4,0},{6,2},{1,5},{3,7},{5,1},{7,3},{8,12},{10,14},{12... | collective-permute-start | bytes 589832 | tf_op jit(solution)/shard_map/ppermute | solution.py:623
  410.7 9.0 %collective-permute-start.22 = (bf16[4,8,3072]{2,1,0:T(8,128)(2,1)S(1)}, bf16[4,8,3072]{2,1,0:T(8,128)(2,1)S(1)}, u32[]{:S(2)}, u32[]{:S(2)}) collective-permute-start(bf16[4,8,3072]{2,1,0:T(8,128)(2,1)S(1)} %get-tuple-element.109), channel_id=1, source_target_pairs={{0,6},{2,0},{4,2},{6,4},{1,7},{3,1},{5,3},{7,5},{8,14},{10,8},{12,... | collective-permute-start | bytes 589832 | tf_op jit(solution)/shard_map/ppermute | solution.py:623
  411.9 8.1 %collective-permute-start.21 = (bf16[4,8,3072]{2,1,0:T(8,128)(2,1)S(1)}, bf16[4,8,3072]{2,1,0:T(8,128)(2,1)S(1)}, u32[]{:S(2)}, u32[]{:S(2)}) collective-permute-start(bf16[4,8,3072]{2,1,0:T(8,128)(2,1)S(1)} %get-tuple-element.107), channel_id=1, source_target_pairs={{0,2},{2,4},{4,6},{6,0},{1,3},{3,5},{5,7},{7,1},{8,10},{10,12},{12... | collective-permute-start | bytes 589832 | tf_op jit(solution)/shard_map/ppermute | solution.py:623
  (66 other events, 502.6 us)
